TPU v7x, 32 devices: a whole 2x2x4 slice. The times are simulated.
32 devices in a mesh: mass: 8 (over z, core), pep: 4 (over y, x).
Axes of the slice: x: 2, y: 2, z: 4, core: 2. Of those that a mesh axis runs over, the one named last changes fastest.
Arguments:
- spectra: bfloat16 [4096, 2048], P('mass'), may hold values from 0 to 2
- peptides: bfloat16 [32768, 2048], P(('mass', 'pep')), may hold values from -0.125 to 0.125
- bounds: int32 [4096, 2], P('mass'), may hold values from 0 to 32767, as said below
Outputs:
- best_score: float32 [4096], P('mass')
Inputs may be any that keep to these rules, and one draw needn't show every extreme that they name: For spectrum i in slab s = i // 512: bounds[i, 0] <= bounds[i, 1]; bounds[i, 0] > (s - 1) * 4096 or is 0; bounds[i, 1] < (s + 2) * 4096; the window holds at least one peptide index of slab s, that is of [s * 4096, (s + 1) * 4096).
All inputs are finite; a program needn't handle non-finite values.
Results may differ from a plain program's by a relative error of at most 0.00085.
Values may be sent and summed in bfloat16 or wider, within the bound.
No kernel may reach another device: no remote copies, remote signals or barrier semaphores. Data moves between devices by JAX's collectives and lax.ppermute only.
A program may use at most 64 MiB of HBM per device.

v0:
```python
import jax
import jax.numpy as jnp
from jax import lax
from jax.sharding import PartitionSpec as P

HALF_TAPS = 75


def with_halo(block, sides, width):
    for axis, dim in sides:
        count = lax.axis_size(axis)
        forward = [(i, i + 1) for i in range(count - 1)]
        backward = [(target, source) for source, target in forward]
        low = lax.ppermute(
            lax.slice_in_dim(block, block.shape[dim] - width, None, axis=dim), axis, forward
        )
        high = lax.ppermute(lax.slice_in_dim(block, 0, width, axis=dim), axis, backward)
        block = jnp.concatenate([low, block, high], axis=dim)
    return block


def process(spectra):
    values = spectra.astype(jnp.float32)
    window_sum = lax.reduce_window(
        values,
        jnp.array(0, values.dtype),
        lax.add,
        (1, 2 * HALF_TAPS + 1),
        (1, 1),
        [(0, 0), (HALF_TAPS, HALF_TAPS)],
    )
    return (values - (window_sum - values) / (2.0 * HALF_TAPS)).astype(jnp.bfloat16)


def masked_best(rows, cands, index, window):
    score = lax.dot_general(
        rows, cands, (((1,), (1,)), ((), ())), preferred_element_type=jnp.float32
    )
    inside = (index[None, :] >= window[:, 0:1]) & (index[None, :] <= window[:, 1:2])
    return jnp.max(jnp.where(inside, score, -1e30), axis=1)


def per_device(spectra, peptides, bounds):
    processed = process(spectra)
    slab = lax.axis_index("mass")
    shard = lax.axis_index("pep")
    shards = lax.axis_size("pep")
    pep_rows = peptides.shape[0]
    extended = with_halo(peptides, (("mass", 0),), pep_rows)
    offset = jnp.arange(3 * pep_rows, dtype=jnp.int32)
    index = ((slab - 1 + offset // pep_rows) * shards + shard) * pep_rows + offset % pep_rows
    local_best = masked_best(processed, extended, index, bounds)
    best_score = lax.pmax(local_best, "pep")
    return best_score


def solution(mesh):
    in_specs = (P("mass", None), P(("mass", "pep"), None), P("mass", None))
    out_specs = P("mass")
    return jax.shard_map(
        per_device, mesh=mesh, in_specs=in_specs, out_specs=out_specs, check_vma=False
    )
```

profile of v0, /device:TPU:1, one launch (start us, length us, event | category | flops | bytes accessed | tf_op | source)
XLA Modules:
  0.0 260.8 jit_solution(6703640169240212708)
XLA Ops:
  0.0 2.0 collective-permute-start.1
  2.0 4.6 %collective-permute-start = (bf16[1024,2048]{1,0:T(8,128)(2,1)}, bf16[1024,2048]{1,0:T(8,128)(2,1)}, u32[]{:S(2)}, u32[]{:S(2)}) collective-permute-start(bf16[1024,2048]{1,0:T(8,128)(2,1)} %param.4), channel_id=1, source_target_pairs={{0,4},{4,8},{8,12},{12,16},{16,20},{20,24},{24,28},{1,5},{5,9},{9,... | collective-permute-start | bytes 12582920 | tf_op jit(solution)/shard_map/ppermute | solution.py:14
  6.5 2.9 %copy.4 = bf16[512,2048]{0,1:T(8,128)(2,1)S(1)} copy(bf16[512,2048]{1,0:T(8,128)(2,1)} %param.3) | data formatting | bytes 4194304 | tf_op args[0]
  9.4 0.0 copy-start
  9.4 227.4 %reduce_window.7 = f32[512,2048]{0,1:T(8,128)} reduce-window(bf16[512,2048]{0,1:T(8,128)(2,1)S(1)} %copy.4, f32[]{:T(128)} %constant.50.clone.1), window={size=1x151 pad=0_0x75_75}, to_apply=%region_0.0 | reduce-window | flops 157286400 | bytes 6291460 | tf_op jit(solution)/shard_map/reduce_window | solution.py:24
  236.8 0.0 copy-done
  236.9 0.0 collective-permute-done.1
  236.9 0.0 collective-permute-done
  236.9 15.2 %select_reduce_fusion = f32[512]{0:T(512)S(1)} fusion(bf16[1024,2048]{1,0:T(8,128)(2,1)} %collective-permute-done.1, bf16[1024,2048]{1,0:T(8,128)(2,1)} %param.4, bf16[1024,2048]{1,0:T(8,128)(2,1)} %collective-permute-done, s32[3072]{0:T(1024)S(1)} %fusion.20, s32[512]{0:T(512)S(1)} %bitcast.3, s32[512]{0:T(512)S(1)} %bitcast.2, ...), kind=kOutput, calls=%fused_computation.6 | convolution fusion | flops 6493306368 | bytes 18892800 | tf_op jit(solution)/shard_map/dot_general | solution.py:36
  252.1 8.5 %pmax.7 = f32[512]{0:T(512)} all-reduce(f32[512]{0:T(512)S(1)} %select_reduce_fusion), channel_id=1, replica_groups=mesh['mass'=8,'pep'=4] {'pep'}, use_global_device_ids=true, to_apply=%region_2.3 | all-reduce | flops 512 | bytes 4096 | tf_op jit(solution)/shard_map/pmax | solution.py:53
  (2 shorter events, 0.0 us)
Async XLA Ops:
  0.0 236.9 %collective-permute-start.1 = (bf16[1024,2048]{1,0:T(8,128)(2,1)}, bf16[1024,2048]{1,0:T(8,128)(2,1)}, u32[]{:S(2)}, u32[]{:S(2)}) collective-permute-start(bf16[1024,2048]{1,0:T(8,128)(2,1)} %param.4), channel_id=1, source_target_pairs={{4,0},{8,4},{12,8},{16,12},{20,16},{24,20},{28,24},{5,1},{9,5},{13... | collective-permute-start | bytes 12582920 | tf_op jit(solution)/shard_map/ppermute | solution.py:17
  2.0 234.9 %collective-permute-start = (bf16[1024,2048]{1,0:T(8,128)(2,1)}, bf16[1024,2048]{1,0:T(8,128)(2,1)}, u32[]{:S(2)}, u32[]{:S(2)}) collective-permute-start(bf16[1024,2048]{1,0:T(8,128)(2,1)} %param.4), channel_id=1, source_target_pairs={{0,4},{4,8},{8,12},{12,16},{16,20},{20,24},{24,28},{1,5},{5,9},{9,... | collective-permute-start | bytes 12582920 | tf_op jit(solution)/shard_map/ppermute | solution.py:14
  9.4 227.4 %copy-start = (s32[512,2]{0,1:T(2,128)S(1)}, s32[512,2]{0,1:T(2,128)}, u32[]{:S(2)}) copy-start(s32[512,2]{0,1:T(2,128)} %param.5) | copy-start | bytes 12292
where the time goes:
time: 265 us; the launch traced here: 261 us
  other arithmetic  227 us (86%)
  matrix products  15.2 us (6%)
  blocking collectives  8.46 us (3%)
  starting transfers between devices  6.51 us (2%)
  local copies, waits for them, and re-layouts  2.88 us (1%)
    another operation x1, other arithmetic, process(): lax.reduce_window(values, jnp.array(0, values.dtype), lax.add, (1, 2 * HA...  227 us
    dot_general x1, matrix products, masked_best(): lax.dot_general(rows, cands, (((1,), (1,)), ((), ())), preferred_element_...  15.2 us
    pmax x1, blocking collectives, per_device(): best_score = lax.pmax(local_best, 'pep')  8.46 us
  transfers between devices with their start and end apart: 2, of which 0 were waited for; matrix products, arithmetic and copies ran while one was open for 88% of the time, Pallas kernels for 0%

commit v1 on v0

v1 whole, which is shorter than its diff:
```python
import functools

import jax
import jax.numpy as jnp
from jax import lax
from jax.experimental import pallas as pl
from jax.experimental.pallas import tpu as pltpu
from jax.sharding import PartitionSpec as P

HALF_TAPS = 75
LOWEST = -1e30
ROW_BY_ROW = (((1,), (1,)), ((), ()))
VMEM = pl.BlockSpec(memory_space=pltpu.VMEM)
SMEM = pl.BlockSpec(memory_space=pltpu.SMEM)
BLOCK = 256
PAD = 128


def process_into(rows_ref, out_ref):
    bins = rows_ref.shape[1]
    source = lax.broadcasted_iota(jnp.int32, (BLOCK + 2 * PAD, BLOCK), 0) - PAD
    target = lax.broadcasted_iota(jnp.int32, (BLOCK + 2 * PAD, BLOCK), 1)
    band = jnp.where(jnp.abs(source - target) <= HALF_TAPS, 1.0, 0.0).astype(jnp.bfloat16)
    for start in range(0, bins, BLOCK):
        low, high = max(start - PAD, 0), min(start + BLOCK + PAD, bins)
        skip = low - (start - PAD)
        window_sum = jnp.dot(
            rows_ref[:, low:high],
            band[skip : skip + high - low],
            preferred_element_type=jnp.float32,
        )
        values = rows_ref[:, start : start + BLOCK].astype(jnp.float32)
        out_ref[:, start : start + BLOCK] = (
            values - (window_sum - values) * (1.0 / (2.0 * HALF_TAPS))
        ).astype(jnp.bfloat16)


def best_of(processed, peptides_ref, bounds, first):
    score = lax.dot_general(
        peptides_ref[...], processed, ROW_BY_ROW, preferred_element_type=jnp.float32
    )
    index = lax.broadcasted_iota(jnp.int32, score.shape, 0)
    inside = (index >= bounds[0:1, :] - first) & (index <= bounds[1:2, :] - first)
    return jnp.max(jnp.where(inside, score, LOWEST), axis=0, keepdims=True)


def score_kernel(place_ref, rows_ref, peptides_ref, bounds_ref, best_ref, processed):
    process_into(rows_ref, processed)
    best_ref[...] = best_of(processed[...], peptides_ref, bounds_ref[...], place_ref[0])


def last_kernel(
    place_ref, rows_ref, peptides_ref, bounds_ref, own_ref, back_ref, out_ref, processed, far
):
    far[...] = jnp.full(far.shape, LOWEST, jnp.float32)

    @pl.when(place_ref[1] > 0)
    def _():
        process_into(rows_ref, processed)
        far[...] = best_of(processed[...], peptides_ref, bounds_ref[...], place_ref[0])

    near = jnp.maximum(own_ref[...], back_ref[...])
    half = (out_ref.shape[0] // 2, out_ref.shape[1])
    lower = place_ref[2] > 0
    out_ref[: half[0]] = jnp.broadcast_to(jnp.where(lower, near, far[...]), half)
    out_ref[half[0] :] = jnp.broadcast_to(jnp.where(lower, far[...], near), half)


def cost(rows, peptides):
    bins = peptides.shape[1]
    return pl.CostEstimate(
        flops=2 * rows * bins * (peptides.shape[0] + BLOCK + 2 * PAD),
        bytes_accessed=2 * bins * (peptides.shape[0] + rows),
        transcendentals=0,
    )


def per_device(spectra, peptides, bounds):
    slabs, shards = lax.axis_size("mass"), lax.axis_size("pep")
    slab, shard = lax.axis_index("mass"), lax.axis_index("pep")
    rows, bins = spectra.shape
    pep_rows = peptides.shape[0]
    chip = [(i, i ^ 1) for i in range(slabs)]
    pairs = [(i, i + 1) for i in range(1, slabs - 1, 2)]
    across = pairs + [(high, low) for low, high in pairs]
    groups = [
        [i * shards + j for i in pair for j in range(shards)]
        for pair in pairs + [(0, slabs - 1)]
    ]
    edge = (slab == 0) | (slab == slabs - 1)
    lower = (slab == 0) | ((slab % 2 == 1) & (slab < slabs - 1))
    place = jnp.stack(
        [(slab * shards + shard) * pep_rows, 1 - edge.astype(jnp.int32), lower.astype(jnp.int32)]
    ).astype(jnp.int32)
    windows = bounds.T

    far_rows = lax.ppermute(spectra, "mass", across)
    far_windows = lax.ppermute(windows, "mass", across)
    near_rows = lax.ppermute(spectra, "mass", chip)
    near_windows = lax.ppermute(windows, "mass", chip)

    score = pl.pallas_call(
        score_kernel,
        out_shape=jax.ShapeDtypeStruct((1, rows), jnp.float32),
        in_specs=[SMEM, VMEM, VMEM, VMEM],
        out_specs=VMEM,
        scratch_shapes=[pltpu.VMEM((rows, bins), jnp.bfloat16)],
        compiler_params=pltpu.CompilerParams(vmem_limit_bytes=16 * 2**20),
        cost_estimate=cost(rows, peptides),
    )
    own = score(place, spectra, peptides, windows)
    near = score(place, near_rows, peptides, near_windows)
    back = lax.ppermute(near, "mass", chip)
    bests = pl.pallas_call(
        last_kernel,
        out_shape=jax.ShapeDtypeStruct((2 * shards, rows), jnp.float32),
        in_specs=[SMEM, VMEM, VMEM, VMEM, VMEM, VMEM],
        out_specs=VMEM,
        scratch_shapes=[
            pltpu.VMEM((rows, bins), jnp.bfloat16),
            pltpu.VMEM((1, rows), jnp.float32),
        ],
        compiler_params=pltpu.CompilerParams(vmem_limit_bytes=16 * 2**20),
        cost_estimate=cost(rows, peptides),
    )(place, far_rows, peptides, far_windows, own, back)
    bests = lax.all_to_all(bests, ("mass", "pep"), 0, 0, axis_index_groups=groups)
    return jnp.max(bests, axis=0)


def solution(mesh):
    in_specs = (P("mass", None), P(("mass", "pep"), None), P("mass", None))
    out_specs = P("mass")
    return jax.shard_map(
        per_device, mesh=mesh, in_specs=in_specs, out_specs=out_specs, check_vma=False
    )
```

time: 265 us -> 43.5 us (0.16); the launches traced: 261 us -> 43.3 us
  other arithmetic: 227 us -> 0.68 us
  matrix products: 15.2 us -> 0 us
  Pallas kernels: 0 us -> 14.4 us
  waiting for transfers between devices: 0.01 us -> 7.88 us
    another operation x1, other arithmetic: 227 us -> 0.08 us  [per_device(): jnp.stack([(slab * shards + shard) * pep_rows, 1 - edge.astype(jnp.int32)...]
    dot_general x1 -> x0, matrix products: 15.2 us -> none  [masked_best(): lax.dot_general(rows, cands, (((1,), (1,)), ((), ())), preferred_element_...]
    pallas_call x0 -> x3, Pallas kernels: none -> 14.4 us  [the longest x1 5.55 us: per_device(): near = score(place, near_rows, peptides, near_windows)]
    all_to_all x0 -> x1, blocking collectives: none -> 9.75 us  [per_device(): lax.all_to_all(bests, ('mass', 'pep'), 0, 0, axis_index_groups=groups)]
    pmax x1 -> x0, blocking collectives: 8.46 us -> none  [per_device(): best_score = lax.pmax(local_best, 'pep')]
    ppermute x2 -> x5, waiting for transfers between devices: 0.01 us -> 7.88 us  [the longest x1 7.87 us: per_device(): far_windows = lax.ppermute(windows, 'mass', across)]
    ppermute x2 -> x5, starting transfers between devices: 6.51 us -> 8.31 us  [the longest x1 4.53 us: per_device(): far_rows = lax.ppermute(spectra, 'mass', across)]
  transfers between devices with their start and end apart: 2 -> 5, of which waited for: 0 -> 1; matrix products, arithmetic and copies ran while one was open for 88% -> 0% of each run, Pallas kernels for 0% -> 23%
where the time goes in v1:
time: 43.5 us; the launch traced here: 43.3 us
  Pallas kernels  14.4 us (33%)
  blocking collectives  9.75 us (22%)
  starting transfers between devices  8.31 us (19%)
  waiting for transfers between devices  7.88 us (18%)
  local copies, waits for them, and re-layouts  2.22 us (5%)
  other arithmetic  0.68 us (2%)
    all_to_all x1, blocking collectives, per_device(): lax.all_to_all(bests, ('mass', 'pep'), 0, 0, axis_index_groups=groups)  9.75 us
    ppermute x1, waiting for transfers between devices, per_device(): far_windows = lax.ppermute(windows, 'mass', across)  7.87 us
    pallas_call x1, Pallas kernels, per_device(): near = score(place, near_rows, peptides, near_windows)  5.55 us
    ppermute x1, starting transfers between devices, per_device(): far_rows = lax.ppermute(spectra, 'mass', across)  4.53 us
    pallas_call x1, Pallas kernels, per_device(): own = score(place, spectra, peptides, windows)  4.45 us
    pallas_call x1, Pallas kernels, per_device(): pl.pallas_call(last_kernel, out_shape=jax.ShapeDtypeStruct((2 * shards, r...  4.38 us
    ppermute x1, starting transfers between devices, per_device(): far_windows = lax.ppermute(windows, 'mass', across)  3.57 us
    unnamed x8, local copies, waits for them, and re-layouts  2.2 us
  transfers between devices with their start and end apart: 5, of which 1 were waited for; matrix products, arithmetic and copies ran while one was open for 0% of the time, Pallas kernels for 23%

profile of v1, /device:TPU:1, one launch (start us, length us, event | category | flops | bytes accessed | tf_op | source)
XLA Modules:
  0.0 43.3 jit_solution(5474674941392428956)
XLA Ops:
  0.0 0.1 collective-permute-start.2
  0.1 4.5 %collective-permute-start = (bf16[512,2048]{1,0:T(8,128)(2,1)}, bf16[512,2048]{1,0:T(8,128)(2,1)S(1)}, u32[]{:S(2)}, u32[]{:S(2)}) collective-permute-start(bf16[512,2048]{1,0:T(8,128)(2,1)} %rows_ref.1), channel_id=1, source_target_pairs={{4,8},{12,16},{20,24},{8,4},{16,12},{24,20},{5,9},{13,17},{21,25},... | collective-permute-start | bytes 6291464 | tf_op jit(solution)/shard_map/ppermute | solution.py:97
  4.6 0.1 collective-permute-start.3
  4.7 3.6 %collective-permute-start.1 = (s32[2,512]{1,0:T(2,128)}, s32[2,512]{1,0:T(2,128)S(1)}, u32[]{:S(2)}, u32[]{:S(2)}) collective-permute-start(s32[2,512]{1,0:T(2,128)} %bitcast.7), channel_id=1, source_target_pairs={{4,8},{12,16},{20,24},{8,4},{16,12},{24,20},{5,9},{13,17},{21,25},... | collective-permute-start | bytes 12296 | tf_op jit(solution)/shard_map/ppermute | solution.py:98
  8.3 0.1 pad_add_fusion.place_ref
  8.4 0.0 collective-permute-done.3.bounds_ref
  8.4 0.0 collective-permute-done.2.rows_ref
  8.4 0.0 copy-start
  8.4 2.2 %copy-done = bf16[1024,2048]{1,0:T(8,128)(2,1)S(1)} copy-done((bf16[1024,2048]{1,0:T(8,128)(2,1)S(1)}, bf16[1024,2048]{1,0:T(8,128)(2,1)}, u32[]{:S(2)}) %copy-start) | copy-done | bytes 4194328
  10.6 0.0 copy-start.1
  10.6 0.0 copy-start.2
  10.6 0.0 copy-start.3
  10.6 5.6 %shard_map.38 = f32[1,512]{1,0:T(1,128)S(1)} custom-call(s32[3]{0:T(128)S(1)} %pad_add_fusion.place_ref, bf16[512,2048]{1,0:T(8,128)(2,1)} %collective-permute-done.2.rows_ref, bf16[1024,2048]{1,0:T(8,128)(2,1)S(1)} %copy-done, s32[2,512]{1,0:T(2,128)S(1)} %collective-permute-done.3.bounds_ref), custom_call_target="tpu_custom_call" | custom-call | flops 3221225472 | bytes 6291456 | tf_op jit(solution)/shard_map/pallas_call | solution.py:112
  16.1 0.1 collective-permute-start.4
  16.2 0.0 copy-done.1
  16.2 0.0 copy-done.2
  16.2 0.0 copy-done.3
  16.2 4.5 %shard_map.37.own_ref = f32[1,512]{1,0:T(1,128)S(1)} custom-call(s32[3]{0:T(128)S(1)} %pad_add_fusion.place_ref, bf16[512,2048]{1,0:T(8,128)(2,1)S(1)} %copy-done.2, bf16[1024,2048]{1,0:T(8,128)(2,1)S(1)} %copy-done.1, s32[2,512]{1,0:T(2,128)S(1)} %bitcast.8), custom_call_target="tpu_custom_call" | custom-call | flops 3221225472 | bytes 6291456 | tf_op jit(solution)/shard_map/pallas_call | solution.py:111
  20.7 7.9 %collective-permute-done.1.bounds_ref = s32[2,512]{1,0:T(2,128)S(1)} collective-permute-done((s32[2,512]{1,0:T(2,128)}, s32[2,512]{1,0:T(2,128)S(1)}, u32[]{:S(2)}, u32[]{:S(2)}) %collective-permute-start.1) | collective-permute-done | bytes 4128 | tf_op jit(solution)/shard_map/ppermute | solution.py:98
  28.6 0.0 collective-permute-done.rows_ref
  28.6 0.0 collective-permute-done.4.back_ref
  28.6 4.4 %shard_map.39 = f32[8,512]{1,0:T(8,128)S(1)} custom-call(s32[3]{0:T(128)S(1)} %pad_add_fusion.place_ref, bf16[512,2048]{1,0:T(8,128)(2,1)S(1)} %collective-permute-done.rows_ref, bf16[1024,2048]{1,0:T(8,128)(2,1)S(1)} %copy-done.1, s32[2,512]{1,0:T(2,128)S(1)} %collective-permute-done.1.bounds_ref, f32[1,512]{1,0:T(1,128)S(1)} %shard_map.37.own_ref, ...), custom_call_target="tpu_custom_call" | custom-call | flops 3221225472 | bytes 6291456 | tf_op jit(solution)/shard_map/pallas_call | solution.py:114
  33.0 9.7 %all_to_all.9 = f32[8,1,512]{2,1,0:T(1,128)S(1)} all-to-all(f32[8,1,512]{2,1,0:T(1,128)S(1)} %copy.4), channel_id=1, replica_groups={{4,5,6,7,8,9,10,11},{12,13,14,15,16,17,18,19},{20,21,22,23,24,25,26,27}..., dimensions={0} | all-to-all | bytes 32768 | tf_op jit(solution)/shard_map/all_to_all | solution.py:126
  42.7 0.6 %reduce_max.9 = f32[512]{0:T(512)} reduce(f32[8,1,512]{2,1,0:T(1,128)S(1)} %all_to_all.9, f32[]{:T(128)} %constant.31.clone.1), dimensions={0,1}, to_apply=%region_0.1 | reduce | flops 3584 | bytes 18436 | tf_op jit(solution)/shard_map/reduce_max | solution.py:127
  (1 shorter events, 0.0 us)
Async XLA Ops:
  0.0 8.4 %collective-permute-start.2 = (bf16[512,2048]{1,0:T(8,128)(2,1)}, bf16[512,2048]{1,0:T(8,128)(2,1)}, u32[]{:S(2)}, u32[]{:S(2)}) collective-permute-start(bf16[512,2048]{1,0:T(8,128)(2,1)} %rows_ref.1), channel_id=1, source_target_pairs={{0,4},{4,0},{8,12},{12,8},{16,20},{20,16},{24,28},{28,24},{1,5},{5... | collective-permute-start | bytes 6291464 | tf_op jit(solution)/shard_map/ppermute | solution.py:99
  0.1 28.5 %collective-permute-start = (bf16[512,2048]{1,0:T(8,128)(2,1)}, bf16[512,2048]{1,0:T(8,128)(2,1)S(1)}, u32[]{:S(2)}, u32[]{:S(2)}) collective-permute-start(bf16[512,2048]{1,0:T(8,128)(2,1)} %rows_ref.1), channel_id=1, source_target_pairs={{4,8},{12,16},{20,24},{8,4},{16,12},{24,20},{5,9},{13,17},{21,25},... | collective-permute-start | bytes 6291464 | tf_op jit(solution)/shard_map/ppermute | solution.py:97
  4.6 3.8 %collective-permute-start.3 = (s32[2,512]{1,0:T(2,128)}, s32[2,512]{1,0:T(2,128)S(1)}, u32[]{:S(2)}, u32[]{:S(2)}) collective-permute-start(s32[2,512]{1,0:T(2,128)} %bitcast.6), channel_id=1, source_target_pairs={{0,4},{4,0},{8,12},{12,8},{16,20},{20,16},{24,28},{28,24},{1,5},{5... | collective-permute-start | bytes 12296 | tf_op jit(solution)/shard_map/ppermute | solution.py:100
  4.7 23.9 %collective-permute-start.1 = (s32[2,512]{1,0:T(2,128)}, s32[2,512]{1,0:T(2,128)S(1)}, u32[]{:S(2)}, u32[]{:S(2)}) collective-permute-start(s32[2,512]{1,0:T(2,128)} %bitcast.7), channel_id=1, source_target_pairs={{4,8},{12,16},{20,24},{8,4},{16,12},{24,20},{5,9},{13,17},{21,25},... | collective-permute-start | bytes 12296 | tf_op jit(solution)/shard_map/ppermute | solution.py:98
  8.4 2.2 %copy-start = (bf16[1024,2048]{1,0:T(8,128)(2,1)S(1)}, bf16[1024,2048]{1,0:T(8,128)(2,1)}, u32[]{:S(2)}) copy-start(bf16[1024,2048]{1,0:T(8,128)(2,1)} %peptides_ref.5) | copy-start | bytes 12582916
  10.6 5.6 %copy-start.1 = (bf16[1024,2048]{1,0:T(8,128)(2,1)S(1)}, bf16[1024,2048]{1,0:T(8,128)(2,1)}, u32[]{:S(2)}) copy-start(bf16[1024,2048]{1,0:T(8,128)(2,1)} %peptides_ref.5) | copy-start | bytes 12582916
  10.6 5.7 %copy-start.2 = (bf16[512,2048]{1,0:T(8,128)(2,1)S(1)}, bf16[512,2048]{1,0:T(8,128)(2,1)}, u32[]{:S(2)}) copy-start(bf16[512,2048]{1,0:T(8,128)(2,1)} %rows_ref.1) | copy-start | bytes 6291460
  10.6 5.7 %copy-start.3 = (s32[512,2]{0,1:T(2,128)S(1)}, s32[512,2]{0,1:T(2,128)}, u32[]{:S(2)}) copy-start(s32[512,2]{0,1:T(2,128)} %param.5) | copy-start | bytes 12292
  16.1 12.4 %collective-permute-start.4 = (f32[1,512]{1,0:T(1,128)S(1)}, f32[1,512]{1,0:T(1,128)S(1)}, u32[]{:S(2)}, u32[]{:S(2)}) collective-permute-start(f32[1,512]{1,0:T(1,128)S(1)} %shard_map.38), channel_id=1, source_target_pairs={{0,4},{4,0},{8,12},{12,8},{16,20},{20,16},{24,28},{28,24},{1,5},{5... | collective-permute-start | bytes 6152 | tf_op jit(solution)/shard_map/ppermute | solution.py:113

commit v2 on v1

v2 whole, which is shorter than its diff:
```python
import jax
import jax.numpy as jnp
from jax import lax
from jax.experimental import pallas as pl
from jax.experimental.pallas import tpu as pltpu
from jax.sharding import PartitionSpec as P

HALF_TAPS = 75
LOWEST = -1e30
ROW_BY_ROW = (((1,), (1,)), ((), ()))
VMEM = pl.BlockSpec(memory_space=pltpu.VMEM)
SMEM = pl.BlockSpec(memory_space=pltpu.SMEM)
HBM = pl.BlockSpec(memory_space=pltpu.HBM)
BLOCK = 256
PAD = 128
NOTE = 16
LONG = 2**35
DIGITS = 3


def process_into(rows_ref, out_ref):
    bins = rows_ref.shape[1]
    source = lax.broadcasted_iota(jnp.int32, (BLOCK + 2 * PAD, BLOCK), 0) - PAD
    target = lax.broadcasted_iota(jnp.int32, (BLOCK + 2 * PAD, BLOCK), 1)
    band = jnp.where(jnp.abs(source - target) <= HALF_TAPS, 1.0, 0.0).astype(jnp.bfloat16)
    for start in range(0, bins, BLOCK):
        low, high = max(start - PAD, 0), min(start + BLOCK + PAD, bins)
        skip = low - (start - PAD)
        window_sum = jnp.dot(
            rows_ref[:, low:high],
            band[skip : skip + high - low],
            preferred_element_type=jnp.float32,
        )
        values = rows_ref[:, start : start + BLOCK].astype(jnp.float32)
        out_ref[:, start : start + BLOCK] = (
            values - (window_sum - values) * (1.0 / (2.0 * HALF_TAPS))
        ).astype(jnp.bfloat16)


def best_of(processed, peptides, bounds, first):
    score = lax.dot_general(peptides, processed, ROW_BY_ROW, preferred_element_type=jnp.float32)
    index = lax.broadcasted_iota(jnp.int32, score.shape, 0)
    inside = (index >= bounds[0] - first) & (index <= bounds[1] - first)
    return jnp.max(jnp.where(inside, score, LOWEST), axis=0, keepdims=True)


def write_note(note_ref, bounds_ref):
    rows = bounds_ref.shape[1]
    row = lax.broadcasted_iota(jnp.int32, (NOTE, rows), 0)
    note = jnp.zeros((NOTE, rows), jnp.int32)
    for k in range(2):
        for d in range(DIGITS):
            digit = (bounds_ref[k : k + 1, :] >> (8 * d)) & 255
            note = jnp.where(row == k * DIGITS + d, digit, note)
    note_ref[...] = jnp.zeros(note_ref.shape, note_ref.dtype)
    note_ref[:, :rows] = note.astype(jnp.float32).astype(note_ref.dtype)


def read_note(note_ref, rows):
    note = note_ref[:, :rows].astype(jnp.float32).astype(jnp.int32)
    return [
        sum(note[k * DIGITS + d : k * DIGITS + d + 1, :] << (8 * d) for d in range(DIGITS))
        for k in range(2)
    ]


def quarter_kernel(place_ref, spectra_ref, quarter_ref, sem):
    part = quarter_ref.shape[0]
    start = pl.multiple_of(place_ref[3] * (spectra_ref.shape[0] - part), 16)
    copy = pltpu.make_async_copy(spectra_ref.at[pl.ds(start, part)], quarter_ref, sem)
    copy.start()
    copy.wait()


def prepare_kernel(
    spectra_ref, bounds_ref, peptides_ref, middle_ref, whole_ref, held_ref, raw, windows, sems
):
    rows = spectra_ref.shape[0]
    half = rows // 2
    count = middle_ref.shape[0] - NOTE
    part = (rows - count) // 2
    sources = [
        (spectra_ref.at[:half], raw.at[:half]),
        (spectra_ref.at[half:], raw.at[half:]),
        (bounds_ref, windows),
        (spectra_ref.at[part : part + count], middle_ref.at[:count]),
        (peptides_ref, held_ref),
    ]
    copies = [
        pltpu.make_async_copy(source, target, sems.at[i])
        for i, (source, target) in enumerate(sources)
    ]
    for copy in copies:
        copy.start()
    copies[0].wait()
    process_into(raw.at[:half], whole_ref.at[:half])
    copies[1].wait()
    process_into(raw.at[half:], whole_ref.at[half:rows])
    copies[2].wait()
    write_note(whole_ref.at[rows:], windows)
    write_note(middle_ref.at[count:], windows)
    copies[3].wait()
    copies[4].wait()


def near_kernel(place_ref, whole_ref, peptides_ref, best_ref):
    rows = best_ref.shape[1]
    bounds = read_note(whole_ref.at[rows:], rows)
    best_ref[...] = best_of(whole_ref[:rows, :], peptides_ref[...], bounds, place_ref[0])


def process_kernel(rows_ref, processed_ref):
    process_into(rows_ref, processed_ref)


def last_kernel(
    place_ref,
    direct_ref,
    relayed_ref,
    far_ref,
    peptides_ref,
    own_ref,
    back_ref,
    out_ref,
    processed,
    far_best,
):
    part = direct_ref.shape[0]
    rows = own_ref.shape[1]
    far_best[...] = jnp.full(far_best.shape, LOWEST, jnp.float32)

    @pl.when(place_ref[1] > 0)
    def _():
        odd = place_ref[3]
        start = pl.multiple_of(odd * (rows - part), part)
        other = pl.multiple_of((1 - odd) * (rows - part), part)
        processed[pl.ds(start, part), :] = direct_ref[...]
        process_into(relayed_ref, processed.at[pl.ds(other, part)])
        process_into(far_ref.at[: rows - 2 * part], processed.at[part : rows - part])
        bounds = read_note(far_ref.at[rows - 2 * part :], rows)
        far_best[...] = best_of(processed[...], peptides_ref[...], bounds, place_ref[0])

    near = jnp.maximum(own_ref[...], back_ref[...])
    half = (out_ref.shape[0] // 2, rows)
    lower = place_ref[2] > 0
    out_ref[: half[0]] = jnp.broadcast_to(jnp.where(lower, near, far_best[...]), half)
    out_ref[half[0] :] = jnp.broadcast_to(jnp.where(lower, far_best[...], near), half)


def in_hbm(array):
    return pltpu.with_memory_space_constraint(array, pltpu.HBM)


def call(kernel, out_shapes, in_specs, scratch, flops=1024):
    return pl.pallas_call(
        kernel,
        out_shape=[jax.ShapeDtypeStruct(shape, dtype) for shape, dtype in out_shapes],
        in_specs=in_specs,
        out_specs=[VMEM] * len(out_shapes),
        scratch_shapes=scratch,
        compiler_params=pltpu.CompilerParams(vmem_limit_bytes=20 * 2**20),
        cost_estimate=pl.CostEstimate(flops=flops, bytes_accessed=1024, transcendentals=0),
    )


def per_device(spectra, peptides, bounds):
    slabs, shards = lax.axis_size("mass"), lax.axis_size("pep")
    slab, shard = lax.axis_index("mass"), lax.axis_index("pep")
    rows, bins = spectra.shape
    pep_rows = peptides.shape[0]
    part = rows // 4
    bf16, f32 = jnp.bfloat16, jnp.float32
    chip = [(i, i ^ 1) for i in range(slabs)]
    pairs = [(i, i + 1) for i in range(1, slabs - 1, 2)]
    across = pairs + [(high, low) for low, high in pairs]
    groups = [
        [i * shards + j for i in pair for j in range(shards)]
        for pair in pairs + [(0, slabs - 1)]
    ]
    beside = (1, shards // 2)
    relay = [
        (i * shards + j, i * shards + (j ^ beside[i % 2]))
        for i in range(1, slabs - 1)
        for j in range(shards)
    ]
    odd = (shard // beside[0] + shard // beside[1]) % 2
    edge = (slab == 0) | (slab == slabs - 1)
    lower = (slab == 0) | ((slab % 2 == 1) & (slab < slabs - 1))
    place = jnp.stack(
        [
            (slab * shards + shard) * pep_rows,
            1 - edge.astype(jnp.int32),
            lower.astype(jnp.int32),
            odd,
        ]
    ).astype(jnp.int32)
    windows = bounds.T

    spectra, windows, peptides = in_hbm(spectra), in_hbm(windows), in_hbm(peptides)

    (quarter,) = call(
        quarter_kernel,
        [((part, bins), bf16)],
        [SMEM, HBM],
        [pltpu.SemaphoreType.DMA],
    )(place, spectra)
    direct = lax.ppermute(quarter, "mass", across)

    quarter, windows = lax.optimization_barrier((quarter, windows))
    middle, whole, held = call(
        prepare_kernel,
        [
            ((rows - 2 * part + NOTE, bins), bf16),
            ((rows + NOTE, bins), bf16),
            (peptides.shape, bf16),
        ],
        [HBM, HBM, HBM],
        [
            pltpu.VMEM((rows, bins), bf16),
            pltpu.VMEM(windows.shape, jnp.int32),
            pltpu.SemaphoreType.DMA((5,)),
        ],
    )(spectra, in_hbm(windows), peptides)
    far = lax.ppermute(middle, "mass", across)
    score = [((1, rows), f32)], [SMEM, VMEM, VMEM], []
    (own_best,) = call(near_kernel, *score)(place, whole, held)

    direct, whole, own_best = lax.optimization_barrier((direct, whole, own_best))
    near = lax.ppermute(whole, "mass", chip)
    relayed = lax.ppermute(direct, ("mass", "pep"), relay)
    (direct,) = call(process_kernel, [((part, bins), bf16)], [VMEM], [], LONG)(direct)
    near, direct = lax.optimization_barrier((near, direct))
    (near_best,) = call(near_kernel, *score)(place, near, held)
    back = lax.ppermute(near_best, "mass", chip)

    (bests,) = call(
        last_kernel,
        [((2 * shards, rows), f32)],
        [SMEM] + [VMEM] * 6,
        [pltpu.VMEM((rows, bins), bf16), pltpu.VMEM((1, rows), f32)],
    )(place, direct, relayed, far, held, own_best, back)
    bests = lax.all_to_all(bests, ("mass", "pep"), 0, 0, axis_index_groups=groups)
    return jnp.max(bests, axis=0)


def solution(mesh):
    in_specs = (P("mass", None), P(("mass", "pep"), None), P("mass", None))
    out_specs = P("mass")
    return jax.shard_map(
        per_device, mesh=mesh, in_specs=in_specs, out_specs=out_specs, check_vma=False
    )
```

time: 43.5 us -> 40.5 us (0.931)
  waiting for transfers between devices: 7.88 us -> 4.77 us
  local copies, waits for them, and re-layouts: 2.22 us -> 0.02 us
  starting transfers between devices: 8.31 us -> 9.94 us
  Pallas kernels: 14.4 us -> 15.6 us
  blocking collectives: 9.75 us -> 9.12 us
    ppermute x5, waiting for transfers between devices: 7.88 us -> 4.77 us  [the longest x1 2.4 us: per_device(): relayed = lax.ppermute(direct, ('mass', 'pep'), relay)]
    unnamed x8 -> x0, local copies, waits for them, and re-layouts: 2.2 us -> none
    ppermute x5, starting transfers between devices: 8.31 us -> 9.94 us  [the longest x1 4.59 us: per_device(): direct = lax.ppermute(quarter, 'mass', across)]
    pallas_call x3 -> x6, Pallas kernels: 14.4 us -> 15.6 us  [the longest x1 4.16 us: per_device(): call(last_kernel, [((2 * shards, rows), f32)], [SMEM] + [VMEM] * 6, [pltp...]
    all_to_all x1, blocking collectives: 9.75 us -> 9.12 us  [per_device(): lax.all_to_all(bests, ('mass', 'pep'), 0, 0, axis_index_groups=groups)]
  transfers between devices with their start and end apart: 5 -> 5, of which waited for: 1 -> 3; matrix products, arithmetic and copies ran while one was open for 0% -> 0% of each run, Pallas kernels for 23% -> 25%
where the time goes in v2:
time: 40.5 us; the launch traced here: 40.2 us
  Pallas kernels  15.6 us (39%)
  starting transfers between devices  9.94 us (25%)
  blocking collectives  9.12 us (23%)
  waiting for transfers between devices  4.77 us (12%)
  other arithmetic  0.68 us (2%)
    all_to_all x1, blocking collectives, per_device(): lax.all_to_all(bests, ('mass', 'pep'), 0, 0, axis_index_groups=groups)  9.12 us
    ppermute x1, starting transfers between devices, per_device(): direct = lax.ppermute(quarter, 'mass', across)  4.59 us
    pallas_call x1, Pallas kernels, per_device(): call(last_kernel, [((2 * shards, rows), f32)], [SMEM] + [VMEM] * 6, [pltp...  4.16 us
    pallas_call x1, Pallas kernels, per_device(): call(prepare_kernel, [((rows - 2 * part + NOTE, bins), bf16), ((rows + NO...  3.22 us
    ppermute x1, starting transfers between devices, per_device(): relayed = lax.ppermute(direct, ('mass', 'pep'), relay)  3.15 us
    pallas_call x1, Pallas kernels, per_device(): own_best, = call(near_kernel, *score)(place, whole, held)  3.08 us
    pallas_call x1, Pallas kernels, per_device(): near_best, = call(near_kernel, *score)(place, near, held)  3.08 us
    ppermute x1, waiting for transfers between devices, per_device(): relayed = lax.ppermute(direct, ('mass', 'pep'), relay)  2.4 us
  transfers between devices with their start and end apart: 5, of which 3 were waited for; matrix products, arithmetic and copies ran while one was open for 0% of the time, Pallas kernels for 25%

profile of v2, /device:TPU:1, one launch (start us, length us, event | category | flops | bytes accessed | tf_op | source)
XLA Modules:
  0.0 40.2 jit_solution(15451750877425836319)
XLA Ops:
  0.0 0.1 pad_add_fusion.place_ref
  0.1 1.6 %shard_map.37 = bf16[128,2048]{1,0:T(8,128)(2,1)S(1)} custom-call(s32[4]{0:T(128)S(1)} %pad_add_fusion.place_ref, bf16[512,2048]{1,0:T(8,128)(2,1)} %spectra_ref.3), custom_call_target="tpu_custom_call" | custom-call | flops 1024 | bytes 1024 | tf_op jit(solution)/shard_map/pallas_call | solution.py:201
  1.7 4.6 %collective-permute-start = (bf16[128,2048]{1,0:T(8,128)(2,1)S(1)}, bf16[128,2048]{1,0:T(8,128)(2,1)S(1)}, u32[]{:S(2)}, u32[]{:S(2)}) collective-permute-start(bf16[128,2048]{1,0:T(8,128)(2,1)S(1)} %shard_map.37), channel_id=1, source_target_pairs={{4,8},{12,16},{20,24},{8,4},{16,12},{24,20},{5,9},{13,17},{21,25},... | collective-permute-start | bytes 1572872 | tf_op jit(solution)/shard_map/ppermute | solution.py:207
  6.3 3.2 %shard_map.38 = (bf16[272,2048]{1,0:T(8,128)(2,1)S(1)}, bf16[528,2048]{1,0:T(8,128)(2,1)S(1)}, bf16[1024,2048]{1,0:T(8,128)(2,1)S(1)}) custom-call(bf16[512,2048]{1,0:T(8,128)(2,1)} %spectra_ref.3, s32[2,512]{1,0:T(2,128)} %bitcast.7, bf16[1024,2048]{1,0:T(8,128)(2,1)} %peptides_ref.1), custom_call_target="tpu_custom_call" | custom-call | flops 1024 | bytes 1024 | tf_op jit(solution)/shard_map/pallas_call | solution.py:210
  9.5 1.9 %collective-permute-start.3 = (bf16[272,2048]{1,0:T(8,128)(2,1)S(1)}, bf16[272,2048]{1,0:T(8,128)(2,1)S(1)}, u32[]{:S(2)}, u32[]{:S(2)}) collective-permute-start(bf16[272,2048]{1,0:T(8,128)(2,1)S(1)} %get-tuple-element.20), channel_id=1, source_target_pairs={{4,8},{12,16},{20,24},{8,4},{16,12},{24,20},{5,9},{13,17},{21,25},... | collective-permute-start | bytes 3342344 | tf_op jit(solution)/shard_map/ppermute | solution.py:224
  11.4 3.1 %shard_map.39.own_ref = f32[1,512]{1,0:T(1,128)S(1)} custom-call(s32[4]{0:T(128)S(1)} %pad_add_fusion.place_ref, bf16[528,2048]{1,0:T(8,128)(2,1)S(1)} %get-tuple-element.17.whole_ref, bf16[1024,2048]{1,0:T(8,128)(2,1)S(1)} %get-tuple-element.16.peptides_ref), custom_call_target="tpu_custom_call" | custom-call | flops 1024 | bytes 1024 | tf_op jit(solution)/shard_map/pallas_call | solution.py:226
  14.5 0.0 collective-permute-done.rows_ref
  14.5 0.1 collective-permute-start.1
  14.6 3.1 %collective-permute-start.2 = (bf16[128,2048]{1,0:T(8,128)(2,1)S(1)}, bf16[128,2048]{1,0:T(8,128)(2,1)S(1)}, u32[]{:S(2)}, u32[]{:S(2)}) collective-permute-start(bf16[128,2048]{1,0:T(8,128)(2,1)S(1)} %collective-permute-done.rows_ref), channel_id=1, source_target_pairs={{4,6},{5,7},{6,4},{7,5},{8,9},{9,8},{10,11},{11,10},{12,14},{13,15... | collective-permute-start | bytes 1572872 | tf_op jit(solution)/shard_map/ppermute | solution.py:230
  17.8 0.5 %shard_map.40.direct_ref = bf16[128,2048]{1,0:T(8,128)(2,1)S(1)} custom-call(bf16[128,2048]{1,0:T(8,128)(2,1)S(1)} %collective-permute-done.rows_ref), custom_call_target="tpu_custom_call" | custom-call | flops 34359738368 | bytes 1024 | tf_op jit(solution)/shard_map/pallas_call | solution.py:231
  18.3 0.6 %collective-permute-done.1.whole_ref = bf16[528,2048]{1,0:T(8,128)(2,1)S(1)} collective-permute-done((bf16[528,2048]{1,0:T(8,128)(2,1)S(1)}, bf16[528,2048]{1,0:T(8,128)(2,1)S(1)}, u32[]{:S(2)}, u32[]{:S(2)}) %collective-permute-start.1) | collective-permute-done | bytes 2162720 | tf_op jit(solution)/shard_map/ppermute | solution.py:229
  18.9 3.1 %shard_map.41 = f32[1,512]{1,0:T(1,128)S(1)} custom-call(s32[4]{0:T(128)S(1)} %pad_add_fusion.place_ref, bf16[528,2048]{1,0:T(8,128)(2,1)S(1)} %collective-permute-done.1.whole_ref, bf16[1024,2048]{1,0:T(8,128)(2,1)S(1)} %get-tuple-element.16.peptides_ref), custom_call_target="tpu_custom_call" | custom-call | flops 1024 | bytes 1024 | tf_op jit(solution)/shard_map/pallas_call | solution.py:233
  21.9 0.2 collective-permute-start.4
  22.1 2.4 %collective-permute-done.2.relayed_ref = bf16[128,2048]{1,0:T(8,128)(2,1)S(1)} collective-permute-done((bf16[128,2048]{1,0:T(8,128)(2,1)S(1)}, bf16[128,2048]{1,0:T(8,128)(2,1)S(1)}, u32[]{:S(2)}, u32[]{:S(2)}) %collective-permute-start.2) | collective-permute-done | bytes 524320 | tf_op jit(solution)/shard_map/ppermute | solution.py:230
  24.5 1.8 %collective-permute-done.3.far_ref = bf16[272,2048]{1,0:T(8,128)(2,1)S(1)} collective-permute-done((bf16[272,2048]{1,0:T(8,128)(2,1)S(1)}, bf16[272,2048]{1,0:T(8,128)(2,1)S(1)}, u32[]{:S(2)}, u32[]{:S(2)}) %collective-permute-start.3) | collective-permute-done | bytes 1114144 | tf_op jit(solution)/shard_map/ppermute | solution.py:224
  26.3 0.0 collective-permute-done.4.back_ref
  26.3 4.2 %shard_map.42 = f32[8,512]{1,0:T(8,128)S(1)} custom-call(s32[4]{0:T(128)S(1)} %pad_add_fusion.place_ref, bf16[128,2048]{1,0:T(8,128)(2,1)S(1)} %shard_map.40.direct_ref, bf16[128,2048]{1,0:T(8,128)(2,1)S(1)} %collective-permute-done.2.relayed_ref, bf16[272,2048]{1,0:T(8,128)(2,1)S(1)} %collective-permute-done.3.far_ref, ...), custom_call_target="tpu_custom_call" | custom-call | flops 1024 | bytes 1024 | tf_op jit(solution)/shard_map/pallas_call | solution.py:236
  30.5 9.1 %all_to_all.9 = f32[8,1,512]{2,1,0:T(1,128)S(1)} all-to-all(f32[8,1,512]{2,1,0:T(1,128)S(1)} %copy.4), channel_id=1, replica_groups={{4,5,6,7,8,9,10,11},{12,13,14,15,16,17,18,19},{20,21,22,23,24,25,26,27}..., dimensions={0} | all-to-all | bytes 32768 | tf_op jit(solution)/shard_map/all_to_all | solution.py:242
  39.6 0.6 %reduce_max.9 = f32[512]{0:T(512)} reduce(f32[8,1,512]{2,1,0:T(1,128)S(1)} %all_to_all.9, f32[]{:T(128)} %constant.54.clone.1), dimensions={0,1}, to_apply=%region_0.1 | reduce | flops 3584 | bytes 18436 | tf_op jit(solution)/shard_map/reduce_max | solution.py:243
  (1 shorter events, 0.0 us)
Async XLA Ops:
  1.7 12.8 %collective-permute-start = (bf16[128,2048]{1,0:T(8,128)(2,1)S(1)}, bf16[128,2048]{1,0:T(8,128)(2,1)S(1)}, u32[]{:S(2)}, u32[]{:S(2)}) collective-permute-start(bf16[128,2048]{1,0:T(8,128)(2,1)S(1)} %shard_map.37), channel_id=1, source_target_pairs={{4,8},{12,16},{20,24},{8,4},{16,12},{24,20},{5,9},{13,17},{21,25},... | collective-permute-start | bytes 1572872 | tf_op jit(solution)/shard_map/ppermute | solution.py:207
  9.5 16.8 %collective-permute-start.3 = (bf16[272,2048]{1,0:T(8,128)(2,1)S(1)}, bf16[272,2048]{1,0:T(8,128)(2,1)S(1)}, u32[]{:S(2)}, u32[]{:S(2)}) collective-permute-start(bf16[272,2048]{1,0:T(8,128)(2,1)S(1)} %get-tuple-element.20), channel_id=1, source_target_pairs={{4,8},{12,16},{20,24},{8,4},{16,12},{24,20},{5,9},{13,17},{21,25},... | collective-permute-start | bytes 3342344 | tf_op jit(solution)/shard_map/ppermute | solution.py:224
  14.5 4.3 %collective-permute-start.1 = (bf16[528,2048]{1,0:T(8,128)(2,1)S(1)}, bf16[528,2048]{1,0:T(8,128)(2,1)S(1)}, u32[]{:S(2)}, u32[]{:S(2)}) collective-permute-start(bf16[528,2048]{1,0:T(8,128)(2,1)S(1)} %get-tuple-element.17.whole_ref), channel_id=1, source_target_pairs={{0,4},{4,0},{8,12},{12,8},{16,20},{20,16},{24,28},{28,24},{1,5},{5... | collective-permute-start | bytes 6488072 | tf_op jit(solution)/shard_map/ppermute | solution.py:229
  14.6 9.9 %collective-permute-start.2 = (bf16[128,2048]{1,0:T(8,128)(2,1)S(1)}, bf16[128,2048]{1,0:T(8,128)(2,1)S(1)}, u32[]{:S(2)}, u32[]{:S(2)}) collective-permute-start(bf16[128,2048]{1,0:T(8,128)(2,1)S(1)} %collective-permute-done.rows_ref), channel_id=1, source_target_pairs={{4,6},{5,7},{6,4},{7,5},{8,9},{9,8},{10,11},{11,10},{12,14},{13,15... | collective-permute-start | bytes 1572872 | tf_op jit(solution)/shard_map/ppermute | solution.py:230
  21.9 4.4 %collective-permute-start.4 = (f32[1,512]{1,0:T(1,128)S(1)}, f32[1,512]{1,0:T(1,128)S(1)}, u32[]{:S(2)}, u32[]{:S(2)}) collective-permute-start(f32[1,512]{1,0:T(1,128)S(1)} %shard_map.41), channel_id=1, source_target_pairs={{0,4},{4,0},{8,12},{12,8},{16,20},{20,16},{24,28},{28,24},{1,5},{5... | collective-permute-start | bytes 6152 | tf_op jit(solution)/shard_map/ppermute | solution.py:234

commit v3 on v2

v3 whole, which is shorter than its diff:
```python
import jax
import jax.numpy as jnp
from jax import lax
from jax.experimental import pallas as pl
from jax.experimental.pallas import tpu as pltpu
from jax.sharding import PartitionSpec as P

HALF_TAPS = 75
LOWEST = -1e30
ROW_BY_ROW = (((1,), (1,)), ((), ()))
VMEM = pl.BlockSpec(memory_space=pltpu.VMEM)
HBM = pl.BlockSpec(memory_space=pltpu.HBM)
BLOCK = 256
PAD = 128
NOTE = 16
LONG = 2**35
DIGITS = 3


def beside(shards):
    return 1, shards // 2


def place(peptides_ref):
    slabs, shards = lax.axis_size("mass"), lax.axis_size("pep")
    slab, shard = lax.axis_index("mass"), lax.axis_index("pep")
    inner = (slab > 0) & (slab < slabs - 1)
    lower = (slab == 0) | ((slab % 2 == 1) & inner)
    odd = (shard // beside(shards)[0] + shard // beside(shards)[1]) % 2
    return (slab * shards + shard) * peptides_ref.shape[0], inner, lower, odd


def process_into(rows_ref, out_ref):
    bins = rows_ref.shape[1]
    source = lax.broadcasted_iota(jnp.int32, (BLOCK + 2 * PAD, BLOCK), 0) - PAD
    target = lax.broadcasted_iota(jnp.int32, (BLOCK + 2 * PAD, BLOCK), 1)
    band = jnp.where(jnp.abs(source - target) <= HALF_TAPS, 1.0, 0.0).astype(jnp.bfloat16)
    for start in range(0, bins, BLOCK):
        low, high = max(start - PAD, 0), min(start + BLOCK + PAD, bins)
        skip = low - (start - PAD)
        window_sum = jnp.dot(
            rows_ref[:, low:high],
            band[skip : skip + high - low],
            preferred_element_type=jnp.float32,
        )
        values = rows_ref[:, start : start + BLOCK].astype(jnp.float32)
        out_ref[:, start : start + BLOCK] = (
            values - (window_sum - values) * (1.0 / (2.0 * HALF_TAPS))
        ).astype(jnp.bfloat16)


def best_of(processed, peptides, bounds, first):
    score = lax.dot_general(peptides, processed, ROW_BY_ROW, preferred_element_type=jnp.float32)
    index = lax.broadcasted_iota(jnp.int32, score.shape, 0)
    inside = (index >= bounds[0] - first) & (index <= bounds[1] - first)
    return jnp.max(jnp.where(inside, score, LOWEST), axis=0, keepdims=True)


def write_note(note_ref, bounds_ref):
    rows = bounds_ref.shape[1]
    row = lax.broadcasted_iota(jnp.int32, (NOTE, rows), 0)
    note = jnp.zeros((NOTE, rows), jnp.int32)
    for k in range(2):
        for d in range(DIGITS):
            digit = (bounds_ref[k : k + 1, :] >> (8 * d)) & 255
            note = jnp.where(row == k * DIGITS + d, digit, note)
    note_ref[...] = jnp.zeros(note_ref.shape, note_ref.dtype)
    note_ref[:, :rows] = note.astype(jnp.float32).astype(note_ref.dtype)


def read_note(note_ref, rows):
    note = note_ref[:, :rows].astype(jnp.float32).astype(jnp.int32)
    return [
        sum(note[k * DIGITS + d : k * DIGITS + d + 1, :] << (8 * d) for d in range(DIGITS))
        for k in range(2)
    ]


def quarter_kernel(spectra_ref, quarter_ref, raw, sems):
    part = quarter_ref.shape[0]
    start = place(spectra_ref)[3] * (spectra_ref.shape[0] - part)
    step = part // sems.shape[0]
    cuts = [(i * step, step) for i in range(sems.shape[0])]
    copies = [
        pltpu.make_async_copy(
            spectra_ref.at[pl.ds(pl.multiple_of(start + low, 16), size)],
            raw.at[low : low + size],
            sems.at[i],
        )
        for i, (low, size) in enumerate(cuts)
    ]
    for copy in copies:
        copy.start()
    for copy in copies:
        copy.wait()
    process_into(raw, quarter_ref)


def middle_kernel(spectra_ref, bounds_ref, middle_ref, raw, windows, sems):
    count = raw.shape[0]
    part = (spectra_ref.shape[0] - count) // 2
    rows = pltpu.make_async_copy(spectra_ref.at[part : part + count], raw, sems.at[0])
    bounds = pltpu.make_async_copy(bounds_ref, windows, sems.at[1])
    bounds.start()
    rows.start()
    bounds.wait()
    write_note(middle_ref.at[count:], windows)
    rows.wait()
    process_into(raw, middle_ref.at[:count])


def whole_kernel(
    spectra_ref, peptides_ref, quarter_ref, middle_ref, whole_ref, held_ref, raw, sems
):
    rows = spectra_ref.shape[0]
    part = quarter_ref.shape[0]
    odd = place(held_ref)[3]
    start = pl.multiple_of(odd * (rows - part), 16)
    other = pl.multiple_of((1 - odd) * (rows - part), 16)
    rest = pltpu.make_async_copy(spectra_ref.at[pl.ds(other, part)], raw, sems.at[0])
    peptides = pltpu.make_async_copy(peptides_ref, held_ref, sems.at[1])
    rest.start()
    peptides.start()
    whole_ref[pl.ds(start, part), :] = quarter_ref[...]
    whole_ref[part : rows - part, :] = middle_ref[: rows - 2 * part, :]
    whole_ref[rows:, :] = middle_ref[rows - 2 * part :, :]
    rest.wait()
    process_into(raw, whole_ref.at[pl.ds(other, part)])
    peptides.wait()


def near_kernel(whole_ref, peptides_ref, best_ref):
    rows = best_ref.shape[1]
    bounds = read_note(whole_ref.at[rows:], rows)
    best_ref[...] = best_of(whole_ref[:rows, :], peptides_ref[...], bounds, place(peptides_ref)[0])


def last_kernel(
    direct_ref,
    relayed_ref,
    middle_ref,
    peptides_ref,
    own_ref,
    back_ref,
    out_ref,
    outer,
    far_best,
):
    part = direct_ref.shape[0]
    rows = own_ref.shape[1]
    far_best[...] = jnp.full(far_best.shape, LOWEST, jnp.float32)

    @pl.when(place(peptides_ref)[1])
    def _():
        odd = place(peptides_ref)[3]
        outer[pl.ds(pl.multiple_of(odd * part, 16), part), :] = direct_ref[...]
        outer[pl.ds(pl.multiple_of((1 - odd) * part, 16), part), :] = relayed_ref[...]
        count = rows - 2 * part
        bounds = read_note(middle_ref.at[count:], rows)
        first = place(peptides_ref)[0]
        far_best[:, part : part + count] = best_of(
            middle_ref[:count, :],
            peptides_ref[...],
            [bound[:, part : part + count] for bound in bounds],
            first,
        )
        ends = [
            jnp.concatenate([bound[:, :part], bound[:, part + count :]], axis=1)
            for bound in bounds
        ]
        best = best_of(outer[...], peptides_ref[...], ends, first)
        far_best[:, :part] = best[:, :part]
        far_best[:, part + count :] = best[:, part:]

    near = jnp.maximum(own_ref[...], back_ref[...])
    half = (out_ref.shape[0] // 2, rows)
    lower = place(peptides_ref)[2]
    out_ref[: half[0]] = jnp.broadcast_to(jnp.where(lower, near, far_best[...]), half)
    out_ref[half[0] :] = jnp.broadcast_to(jnp.where(lower, far_best[...], near), half)


def in_hbm(array):
    return pltpu.with_memory_space_constraint(array, pltpu.HBM)


def call(kernel, out_shapes, in_specs, scratch, flops=1024):
    return pl.pallas_call(
        kernel,
        out_shape=[jax.ShapeDtypeStruct(shape, dtype) for shape, dtype in out_shapes],
        in_specs=in_specs,
        out_specs=[VMEM] * len(out_shapes),
        scratch_shapes=scratch,
        compiler_params=pltpu.CompilerParams(vmem_limit_bytes=20 * 2**20),
        cost_estimate=pl.CostEstimate(flops=flops, bytes_accessed=1024, transcendentals=0),
    )


def per_device(spectra, peptides, bounds):
    slabs, shards = lax.axis_size("mass"), lax.axis_size("pep")
    rows, bins = spectra.shape
    pep_rows = peptides.shape[0]
    part = rows // 4
    bf16, f32 = jnp.bfloat16, jnp.float32
    chip = [(i, i ^ 1) for i in range(slabs)]
    pairs = [(i, i + 1) for i in range(1, slabs - 1, 2)]
    across = pairs + [(high, low) for low, high in pairs]
    groups = [
        [i * shards + j for i in pair for j in range(shards)]
        for pair in pairs + [(0, slabs - 1)]
    ]
    relay = [
        (i * shards + j, i * shards + (j ^ beside(shards)[i % 2]))
        for i in range(1, slabs - 1)
        for j in range(shards)
    ]
    windows = bounds.T

    spectra, windows, peptides = in_hbm(spectra), in_hbm(windows), in_hbm(peptides)

    (quarter,) = call(
        quarter_kernel,
        [((part, bins), bf16)],
        [HBM],
        [pltpu.VMEM((part, bins), bf16), pltpu.SemaphoreType.DMA((2,))],
    )(spectra)
    direct = lax.ppermute(quarter, "mass", across)

    quarter, windows = lax.optimization_barrier((quarter, windows))
    (middle,) = call(
        middle_kernel,
        [((rows - 2 * part + NOTE, bins), bf16)],
        [HBM, HBM],
        [
            pltpu.VMEM((rows - 2 * part, bins), bf16),
            pltpu.VMEM(windows.shape, jnp.int32),
            pltpu.SemaphoreType.DMA((2,)),
        ],
    )(spectra, in_hbm(windows))
    far = lax.ppermute(middle, "mass", across)
    whole, held = call(
        whole_kernel,
        [((rows + NOTE, bins), bf16), (peptides.shape, bf16)],
        [HBM, HBM, VMEM, VMEM],
        [pltpu.VMEM((part, bins), bf16), pltpu.SemaphoreType.DMA((2,))],
    )(spectra, peptides, quarter, middle)

    score = [((1, rows), f32)], [VMEM, VMEM], []
    (own_best,) = call(near_kernel, *score, LONG)(whole, held)
    direct, whole = lax.optimization_barrier((direct, whole))
    near = lax.ppermute(whole, "mass", chip)
    relayed = lax.ppermute(direct, ("mass", "pep"), relay)
    near, own_best = lax.optimization_barrier((near, own_best))
    (near_best,) = call(near_kernel, *score)(near, held)
    back = lax.ppermute(near_best, "mass", chip)

    (bests,) = call(
        last_kernel,
        [((2 * shards, rows), f32)],
        [VMEM] * 6,
        [pltpu.VMEM((2 * part, bins), bf16), pltpu.VMEM((1, rows), f32)],
    )(direct, relayed, far, held, own_best, back)
    bests = lax.all_to_all(bests, ("mass", "pep"), 0, 0, axis_index_groups=groups)
    return jnp.max(bests, axis=0)


def solution(mesh):
    in_specs = (P("mass", None), P(("mass", "pep"), None), P("mass", None))
    out_specs = P("mass")
    return jax.shard_map(
        per_device, mesh=mesh, in_specs=in_specs, out_specs=out_specs, check_vma=False
    )
```

time: 40.5 us -> 38.2 us (0.943)
  Pallas kernels: 15.6 us -> 13.7 us
  waiting for transfers between devices: 4.77 us -> 4.16 us
  blocking collectives: 9.12 us -> 9.67 us
    pallas_call x6, Pallas kernels: 15.6 us -> 13.7 us  [the longest x1 2.62 us: per_device(): call(last_kernel, [((2 * shards, rows), f32)], [VMEM] * 6, [pltpu.VMEM((2...]
    ppermute x1, waiting for transfers between devices: 2.4 us -> 1.58 us  [per_device(): relayed = lax.ppermute(direct, ('mass', 'pep'), relay)]
    ppermute x1, waiting for transfers between devices: 0.58 us -> 0.01 us  [per_device(): near = lax.ppermute(whole, 'mass', chip)]
    all_to_all x1, blocking collectives: 9.12 us -> 9.67 us  [per_device(): lax.all_to_all(bests, ('mass', 'pep'), 0, 0, axis_index_groups=groups)]
    ppermute x1, waiting for transfers between devices: 0.01 us -> 0.48 us  [per_device(): direct = lax.ppermute(quarter, 'mass', across)]
where the time goes in v3:
time: 38.2 us; the launch traced here: 37.9 us
  Pallas kernels  13.7 us (36%)
  starting transfers between devices  9.73 us (25%)
  blocking collectives  9.67 us (25%)
  waiting for transfers between devices  4.16 us (11%)
  other arithmetic  0.61 us (2%)
    all_to_all x1, blocking collectives, per_device(): lax.all_to_all(bests, ('mass', 'pep'), 0, 0, axis_index_groups=groups)  9.67 us
    ppermute x1, starting transfers between devices, per_device(): direct = lax.ppermute(quarter, 'mass', across)  4.59 us
    ppermute x1, starting transfers between devices, per_device(): relayed = lax.ppermute(direct, ('mass', 'pep'), relay)  3.14 us
    pallas_call x1, Pallas kernels, per_device(): call(last_kernel, [((2 * shards, rows), f32)], [VMEM] * 6, [pltpu.VMEM((2...  2.62 us
    pallas_call x1, Pallas kernels, per_device(): near_best, = call(near_kernel, *score)(near, held)  2.54 us
    pallas_call x1, Pallas kernels, per_device(): own_best, = call(near_kernel, *score, LONG)(whole, held)  2.54 us
    pallas_call x1, Pallas kernels, per_device(): call(whole_kernel, [((rows + NOTE, bins), bf16), (peptides.shape, bf16)],...  2.4 us
    ppermute x1, waiting for transfers between devices, per_device(): far = lax.ppermute(middle, 'mass', across)  2.09 us
  transfers between devices with their start and end apart: 5, of which 3 were waited for; matrix products, arithmetic and copies ran while one was open for 0% of the time, Pallas kernels for 25%

profile of v3, /device:TPU:1, one launch (start us, length us, event | category | flops | bytes accessed | tf_op | source)
XLA Modules:
  0.0 37.9 jit_solution(230263555050311781)
XLA Ops:
  0.0 1.5 %shard_map.37.quarter_ref = bf16[128,2048]{1,0:T(8,128)(2,1)S(1)} custom-call(bf16[512,2048]{1,0:T(8,128)(2,1)} %spectra_ref.5), custom_call_target="tpu_custom_call" | custom-call | flops 1024 | bytes 1024 | tf_op jit(solution)/shard_map/pallas_call | solution.py:220
  1.5 4.6 %collective-permute-start = (bf16[128,2048]{1,0:T(8,128)(2,1)S(1)}, bf16[128,2048]{1,0:T(8,128)(2,1)S(1)}, u32[]{:S(2)}, u32[]{:S(2)}) collective-permute-start(bf16[128,2048]{1,0:T(8,128)(2,1)S(1)} %shard_map.37.quarter_ref), channel_id=1, source_target_pairs={{4,8},{12,16},{20,24},{8,4},{16,12},{24,20},{5,9},{13,17},{21,25},... | collective-permute-start | bytes 1572872 | tf_op jit(solution)/shard_map/ppermute | solution.py:226
  6.1 2.0 %shard_map.38.middle_ref = bf16[272,2048]{1,0:T(8,128)(2,1)S(1)} custom-call(bf16[512,2048]{1,0:T(8,128)(2,1)} %spectra_ref.5, s32[2,512]{1,0:T(2,128)} %bitcast.3), custom_call_target="tpu_custom_call" | custom-call | flops 1024 | bytes 1024 | tf_op jit(solution)/shard_map/pallas_call | solution.py:229
  8.2 1.9 %collective-permute-start.2 = (bf16[272,2048]{1,0:T(8,128)(2,1)S(1)}, bf16[272,2048]{1,0:T(8,128)(2,1)S(1)}, u32[]{:S(2)}, u32[]{:S(2)}) collective-permute-start(bf16[272,2048]{1,0:T(8,128)(2,1)S(1)} %shard_map.38.middle_ref), channel_id=1, source_target_pairs={{4,8},{12,16},{20,24},{8,4},{16,12},{24,20},{5,9},{13,17},{21,25},... | collective-permute-start | bytes 3342344 | tf_op jit(solution)/shard_map/ppermute | solution.py:239
  10.1 2.4 %shard_map.39 = (bf16[528,2048]{1,0:T(8,128)(2,1)S(1)}, bf16[1024,2048]{1,0:T(8,128)(2,1)S(1)}) custom-call(bf16[512,2048]{1,0:T(8,128)(2,1)} %spectra_ref.5, bf16[1024,2048]{1,0:T(8,128)(2,1)} %peptides_ref.1, bf16[128,2048]{1,0:T(8,128)(2,1)S(1)} %shard_map.37.quarter_ref, bf16[272,2048]{1,0:T(8,128)(2,1)S(1)} %shard_map.38.middle_ref), custom_call_target="tpu_custom_call" | custom-call | flops 1024 | bytes 1024 | tf_op jit(solution)/shard_map/pallas_call | solution.py:240
  12.5 0.5 %collective-permute-done.direct_ref = bf16[128,2048]{1,0:T(8,128)(2,1)S(1)} collective-permute-done((bf16[128,2048]{1,0:T(8,128)(2,1)S(1)}, bf16[128,2048]{1,0:T(8,128)(2,1)S(1)}, u32[]{:S(2)}, u32[]{:S(2)}) %collective-permute-start) | collective-permute-done | bytes 524320 | tf_op jit(solution)/shard_map/ppermute | solution.py:226
  13.0 0.0 collective-permute-start.3
  13.0 3.1 %collective-permute-start.1 = (bf16[128,2048]{1,0:T(8,128)(2,1)S(1)}, bf16[128,2048]{1,0:T(8,128)(2,1)S(1)}, u32[]{:S(2)}, u32[]{:S(2)}) collective-permute-start(bf16[128,2048]{1,0:T(8,128)(2,1)S(1)} %collective-permute-done.direct_ref), channel_id=1, source_target_pairs={{4,6},{5,7},{6,4},{7,5},{8,9},{9,8},{10,11},{11,10},{12,14},{13,15... | collective-permute-start | bytes 1572872 | tf_op jit(solution)/shard_map/ppermute | solution.py:251
  16.1 2.5 %shard_map.40.own_ref = f32[1,512]{1,0:T(1,128)S(1)} custom-call(bf16[528,2048]{1,0:T(8,128)(2,1)S(1)} %get-tuple-element.18.whole_ref, bf16[1024,2048]{1,0:T(8,128)(2,1)S(1)} %get-tuple-element.17.peptides_ref), custom_call_target="tpu_custom_call" | custom-call | flops 34359738368 | bytes 1024 | tf_op jit(solution)/shard_map/pallas_call | solution.py:248
  18.7 0.0 collective-permute-done.3.whole_ref
  18.7 2.5 %shard_map.41 = f32[1,512]{1,0:T(1,128)S(1)} custom-call(bf16[528,2048]{1,0:T(8,128)(2,1)S(1)} %collective-permute-done.3.whole_ref, bf16[1024,2048]{1,0:T(8,128)(2,1)S(1)} %get-tuple-element.17.peptides_ref), custom_call_target="tpu_custom_call" | custom-call | flops 1024 | bytes 1024 | tf_op jit(solution)/shard_map/pallas_call | solution.py:253
  21.2 0.1 collective-permute-start.4
  21.3 1.6 %collective-permute-done.1.relayed_ref = bf16[128,2048]{1,0:T(8,128)(2,1)S(1)} collective-permute-done((bf16[128,2048]{1,0:T(8,128)(2,1)S(1)}, bf16[128,2048]{1,0:T(8,128)(2,1)S(1)}, u32[]{:S(2)}, u32[]{:S(2)}) %collective-permute-start.1) | collective-permute-done | bytes 524320 | tf_op jit(solution)/shard_map/ppermute | solution.py:251
  22.9 2.1 %collective-permute-done.2.middle_ref = bf16[272,2048]{1,0:T(8,128)(2,1)S(1)} collective-permute-done((bf16[272,2048]{1,0:T(8,128)(2,1)S(1)}, bf16[272,2048]{1,0:T(8,128)(2,1)S(1)}, u32[]{:S(2)}, u32[]{:S(2)}) %collective-permute-start.2) | collective-permute-done | bytes 1114144 | tf_op jit(solution)/shard_map/ppermute | solution.py:239
  25.0 0.0 collective-permute-done.4.back_ref
  25.0 2.6 %shard_map.42 = f32[8,512]{1,0:T(8,128)S(1)} custom-call(bf16[128,2048]{1,0:T(8,128)(2,1)S(1)} %collective-permute-done.direct_ref, bf16[128,2048]{1,0:T(8,128)(2,1)S(1)} %collective-permute-done.1.relayed_ref, bf16[272,2048]{1,0:T(8,128)(2,1)S(1)} %collective-permute-done.2.middle_ref, bf16[1024,2048]{1,0:T(8,128)(2,1)S(1)} %get-tuple-element.17.peptides_ref, ...), custom_call_target="tpu_custom_call" | custom-call | flops 1024 | bytes 1024 | tf_op jit(solution)/shard_map/pallas_call | solution.py:256
  27.7 9.7 %all_to_all.9 = f32[8,1,512]{2,1,0:T(1,128)S(1)} all-to-all(f32[8,1,512]{2,1,0:T(1,128)S(1)} %copy.4), channel_id=1, replica_groups={{4,5,6,7,8,9,10,11},{12,13,14,15,16,17,18,19},{20,21,22,23,24,25,26,27}..., dimensions={0} | all-to-all | bytes 32768 | tf_op jit(solution)/shard_map/all_to_all | solution.py:262
  37.3 0.6 %reduce_max.9 = f32[512]{0:T(512)} reduce(f32[8,1,512]{2,1,0:T(1,128)S(1)} %all_to_all.9, f32[]{:T(128)} %constant.0.clone.1), dimensions={0,1}, to_apply=%region_0.0 | reduce | flops 3584 | bytes 18436 | tf_op jit(solution)/shard_map/reduce_max | solution.py:263
  (1 shorter events, 0.0 us)
Async XLA Ops:
  1.5 11.5 %collective-permute-start = (bf16[128,2048]{1,0:T(8,128)(2,1)S(1)}, bf16[128,2048]{1,0:T(8,128)(2,1)S(1)}, u32[]{:S(2)}, u32[]{:S(2)}) collective-permute-start(bf16[128,2048]{1,0:T(8,128)(2,1)S(1)} %shard_map.37.quarter_ref), channel_id=1, source_target_pairs={{4,8},{12,16},{20,24},{8,4},{16,12},{24,20},{5,9},{13,17},{21,25},... | collective-permute-start | bytes 1572872 | tf_op jit(solution)/shard_map/ppermute | solution.py:226
  8.2 16.8 %collective-permute-start.2 = (bf16[272,2048]{1,0:T(8,128)(2,1)S(1)}, bf16[272,2048]{1,0:T(8,128)(2,1)S(1)}, u32[]{:S(2)}, u32[]{:S(2)}) collective-permute-start(bf16[272,2048]{1,0:T(8,128)(2,1)S(1)} %shard_map.38.middle_ref), channel_id=1, source_target_pairs={{4,8},{12,16},{20,24},{8,4},{16,12},{24,20},{5,9},{13,17},{21,25},... | collective-permute-start | bytes 3342344 | tf_op jit(solution)/shard_map/ppermute | solution.py:239
  13.0 5.7 %collective-permute-start.3 = (bf16[528,2048]{1,0:T(8,128)(2,1)S(1)}, bf16[528,2048]{1,0:T(8,128)(2,1)S(1)}, u32[]{:S(2)}, u32[]{:S(2)}) collective-permute-start(bf16[528,2048]{1,0:T(8,128)(2,1)S(1)} %get-tuple-element.18.whole_ref), channel_id=1, source_target_pairs={{0,4},{4,0},{8,12},{12,8},{16,20},{20,16},{24,28},{28,24},{1,5},{5... | collective-permute-start | bytes 6488072 | tf_op jit(solution)/shard_map/ppermute | solution.py:250
  13.0 9.9 %collective-permute-start.1 = (bf16[128,2048]{1,0:T(8,128)(2,1)S(1)}, bf16[128,2048]{1,0:T(8,128)(2,1)S(1)}, u32[]{:S(2)}, u32[]{:S(2)}) collective-permute-start(bf16[128,2048]{1,0:T(8,128)(2,1)S(1)} %collective-permute-done.direct_ref), channel_id=1, source_target_pairs={{4,6},{5,7},{6,4},{7,5},{8,9},{9,8},{10,11},{11,10},{12,14},{13,15... | collective-permute-start | bytes 1572872 | tf_op jit(solution)/shard_map/ppermute | solution.py:251
  21.2 3.8 %collective-permute-start.4 = (f32[1,512]{1,0:T(1,128)S(1)}, f32[1,512]{1,0:T(1,128)S(1)}, u32[]{:S(2)}, u32[]{:S(2)}) collective-permute-start(f32[1,512]{1,0:T(1,128)S(1)} %shard_map.41), channel_id=1, source_target_pairs={{0,4},{4,0},{8,12},{12,8},{16,20},{20,16},{24,28},{28,24},{1,5},{5... | collective-permute-start | bytes 6152 | tf_op jit(solution)/shard_map/ppermute | solution.py:254

commit v4 on v3

--- a/solution.py
+++ b/solution.py
@@ -12,7 +12,7 @@
 HBM = pl.BlockSpec(memory_space=pltpu.HBM)
 BLOCK = 256
 PAD = 128
-NOTE = 16
+NOTE = 8
 LONG = 2**35
 DIGITS = 3
 

time: 38.2 us -> 37.8 us (0.990)
  no operation moved by 1% of the time
where the time goes in v4:
time: 37.8 us; the launch traced here: 37.6 us
  Pallas kernels  13.7 us (36%)
  starting transfers between devices  9.73 us (26%)
  blocking collectives  9.68 us (26%)
  waiting for transfers between devices  3.81 us (10%)
  other arithmetic  0.61 us (2%)
    all_to_all x1, blocking collectives, per_device(): lax.all_to_all(bests, ('mass', 'pep'), 0, 0, axis_index_groups=groups)  9.68 us
    ppermute x1, starting transfers between devices, per_device(): direct = lax.ppermute(quarter, 'mass', across)  4.59 us
    ppermute x1, starting transfers between devices, per_device(): relayed = lax.ppermute(direct, ('mass', 'pep'), relay)  3.14 us
    pallas_call x1, Pallas kernels, per_device(): call(last_kernel, [((2 * shards, rows), f32)], [VMEM] * 6, [pltpu.VMEM((2...  2.62 us
    pallas_call x1, Pallas kernels, per_device(): own_best, = call(near_kernel, *score, LONG)(whole, held)  2.54 us
    pallas_call x1, Pallas kernels, per_device(): near_best, = call(near_kernel, *score)(near, held)  2.54 us
    pallas_call x1, Pallas kernels, per_device(): call(whole_kernel, [((rows + NOTE, bins), bf16), (peptides.shape, bf16)],...  2.4 us
    pallas_call x1, Pallas kernels, per_device(): call(middle_kernel, [((rows - 2 * part + NOTE, bins), bf16)], [HBM, HBM],...  2.03 us
  transfers between devices with their start and end apart: 5, of which 3 were waited for; matrix products, arithmetic and copies ran while one was open for 0% of the time, Pallas kernels for 25%

profile of v4, /device:TPU:1, one launch (start us, length us, event | category | flops | bytes accessed | tf_op | source)
XLA Modules:
  0.0 37.6 jit_solution(16393044517579212513)
XLA Ops:
  0.0 1.5 %shard_map.37.quarter_ref = bf16[128,2048]{1,0:T(8,128)(2,1)S(1)} custom-call(bf16[512,2048]{1,0:T(8,128)(2,1)} %spectra_ref.5), custom_call_target="tpu_custom_call" | custom-call | flops 1024 | bytes 1024 | tf_op jit(solution)/shard_map/pallas_call | solution.py:220
  1.5 4.6 %collective-permute-start = (bf16[128,2048]{1,0:T(8,128)(2,1)S(1)}, bf16[128,2048]{1,0:T(8,128)(2,1)S(1)}, u32[]{:S(2)}, u32[]{:S(2)}) collective-permute-start(bf16[128,2048]{1,0:T(8,128)(2,1)S(1)} %shard_map.37.quarter_ref), channel_id=1, source_target_pairs={{4,8},{12,16},{20,24},{8,4},{16,12},{24,20},{5,9},{13,17},{21,25},... | collective-permute-start | bytes 1572872 | tf_op jit(solution)/shard_map/ppermute | solution.py:226
  6.1 2.0 %shard_map.38.middle_ref = bf16[264,2048]{1,0:T(8,128)(2,1)S(1)} custom-call(bf16[512,2048]{1,0:T(8,128)(2,1)} %spectra_ref.5, s32[2,512]{1,0:T(2,128)} %bitcast.3), custom_call_target="tpu_custom_call" | custom-call | flops 1024 | bytes 1024 | tf_op jit(solution)/shard_map/pallas_call | solution.py:229
  8.2 1.9 %collective-permute-start.2 = (bf16[264,2048]{1,0:T(8,128)(2,1)S(1)}, bf16[264,2048]{1,0:T(8,128)(2,1)S(1)}, u32[]{:S(2)}, u32[]{:S(2)}) collective-permute-start(bf16[264,2048]{1,0:T(8,128)(2,1)S(1)} %shard_map.38.middle_ref), channel_id=1, source_target_pairs={{4,8},{12,16},{20,24},{8,4},{16,12},{24,20},{5,9},{13,17},{21,25},... | collective-permute-start | bytes 3244040 | tf_op jit(solution)/shard_map/ppermute | solution.py:239
  10.1 2.4 %shard_map.39 = (bf16[520,2048]{1,0:T(8,128)(2,1)S(1)}, bf16[1024,2048]{1,0:T(8,128)(2,1)S(1)}) custom-call(bf16[512,2048]{1,0:T(8,128)(2,1)} %spectra_ref.5, bf16[1024,2048]{1,0:T(8,128)(2,1)} %peptides_ref.1, bf16[128,2048]{1,0:T(8,128)(2,1)S(1)} %shard_map.37.quarter_ref, bf16[264,2048]{1,0:T(8,128)(2,1)S(1)} %shard_map.38.middle_ref), custom_call_target="tpu_custom_call" | custom-call | flops 1024 | bytes 1024 | tf_op jit(solution)/shard_map/pallas_call | solution.py:240
  12.5 0.5 %collective-permute-done.direct_ref = bf16[128,2048]{1,0:T(8,128)(2,1)S(1)} collective-permute-done((bf16[128,2048]{1,0:T(8,128)(2,1)S(1)}, bf16[128,2048]{1,0:T(8,128)(2,1)S(1)}, u32[]{:S(2)}, u32[]{:S(2)}) %collective-permute-start) | collective-permute-done | bytes 524320 | tf_op jit(solution)/shard_map/ppermute | solution.py:226
  13.0 0.0 collective-permute-start.3
  13.0 3.1 %collective-permute-start.1 = (bf16[128,2048]{1,0:T(8,128)(2,1)S(1)}, bf16[128,2048]{1,0:T(8,128)(2,1)S(1)}, u32[]{:S(2)}, u32[]{:S(2)}) collective-permute-start(bf16[128,2048]{1,0:T(8,128)(2,1)S(1)} %collective-permute-done.direct_ref), channel_id=1, source_target_pairs={{4,6},{5,7},{6,4},{7,5},{8,9},{9,8},{10,11},{11,10},{12,14},{13,15... | collective-permute-start | bytes 1572872 | tf_op jit(solution)/shard_map/ppermute | solution.py:251
  16.1 2.5 %shard_map.40.own_ref = f32[1,512]{1,0:T(1,128)S(1)} custom-call(bf16[520,2048]{1,0:T(8,128)(2,1)S(1)} %get-tuple-element.18.whole_ref, bf16[1024,2048]{1,0:T(8,128)(2,1)S(1)} %get-tuple-element.17.peptides_ref), custom_call_target="tpu_custom_call" | custom-call | flops 34359738368 | bytes 1024 | tf_op jit(solution)/shard_map/pallas_call | solution.py:248
  18.7 0.0 collective-permute-done.3.whole_ref
  18.7 2.5 %shard_map.41 = f32[1,512]{1,0:T(1,128)S(1)} custom-call(bf16[520,2048]{1,0:T(8,128)(2,1)S(1)} %collective-permute-done.3.whole_ref, bf16[1024,2048]{1,0:T(8,128)(2,1)S(1)} %get-tuple-element.17.peptides_ref), custom_call_target="tpu_custom_call" | custom-call | flops 1024 | bytes 1024 | tf_op jit(solution)/shard_map/pallas_call | solution.py:253
  21.2 0.1 collective-permute-start.4
  21.3 1.6 %collective-permute-done.1.relayed_ref = bf16[128,2048]{1,0:T(8,128)(2,1)S(1)} collective-permute-done((bf16[128,2048]{1,0:T(8,128)(2,1)S(1)}, bf16[128,2048]{1,0:T(8,128)(2,1)S(1)}, u32[]{:S(2)}, u32[]{:S(2)}) %collective-permute-start.1) | collective-permute-done | bytes 524320 | tf_op jit(solution)/shard_map/ppermute | solution.py:251
  22.9 1.7 %collective-permute-done.2.middle_ref = bf16[264,2048]{1,0:T(8,128)(2,1)S(1)} collective-permute-done((bf16[264,2048]{1,0:T(8,128)(2,1)S(1)}, bf16[264,2048]{1,0:T(8,128)(2,1)S(1)}, u32[]{:S(2)}, u32[]{:S(2)}) %collective-permute-start.2) | collective-permute-done | bytes 1081376 | tf_op jit(solution)/shard_map/ppermute | solution.py:239
  24.7 0.0 collective-permute-done.4.back_ref
  24.7 2.6 %shard_map.42 = f32[8,512]{1,0:T(8,128)S(1)} custom-call(bf16[128,2048]{1,0:T(8,128)(2,1)S(1)} %collective-permute-done.direct_ref, bf16[128,2048]{1,0:T(8,128)(2,1)S(1)} %collective-permute-done.1.relayed_ref, bf16[264,2048]{1,0:T(8,128)(2,1)S(1)} %collective-permute-done.2.middle_ref, bf16[1024,2048]{1,0:T(8,128)(2,1)S(1)} %get-tuple-element.17.peptides_ref, ...), custom_call_target="tpu_custom_call" | custom-call | flops 1024 | bytes 1024 | tf_op jit(solution)/shard_map/pallas_call | solution.py:256
  27.3 9.7 %all_to_all.9 = f32[8,1,512]{2,1,0:T(1,128)S(1)} all-to-all(f32[8,1,512]{2,1,0:T(1,128)S(1)} %copy.4), channel_id=1, replica_groups={{4,5,6,7,8,9,10,11},{12,13,14,15,16,17,18,19},{20,21,22,23,24,25,26,27}..., dimensions={0} | all-to-all | bytes 32768 | tf_op jit(solution)/shard_map/all_to_all | solution.py:262
  37.0 0.6 %reduce_max.9 = f32[512]{0:T(512)} reduce(f32[8,1,512]{2,1,0:T(1,128)S(1)} %all_to_all.9, f32[]{:T(128)} %constant.0.clone.1), dimensions={0,1}, to_apply=%region_0.0 | reduce | flops 3584 | bytes 18436 | tf_op jit(solution)/shard_map/reduce_max | solution.py:263
  (1 shorter events, 0.0 us)
Async XLA Ops:
  1.5 11.5 %collective-permute-start = (bf16[128,2048]{1,0:T(8,128)(2,1)S(1)}, bf16[128,2048]{1,0:T(8,128)(2,1)S(1)}, u32[]{:S(2)}, u32[]{:S(2)}) collective-permute-start(bf16[128,2048]{1,0:T(8,128)(2,1)S(1)} %shard_map.37.quarter_ref), channel_id=1, source_target_pairs={{4,8},{12,16},{20,24},{8,4},{16,12},{24,20},{5,9},{13,17},{21,25},... | collective-permute-start | bytes 1572872 | tf_op jit(solution)/shard_map/ppermute | solution.py:226
  8.2 16.5 %collective-permute-start.2 = (bf16[264,2048]{1,0:T(8,128)(2,1)S(1)}, bf16[264,2048]{1,0:T(8,128)(2,1)S(1)}, u32[]{:S(2)}, u32[]{:S(2)}) collective-permute-start(bf16[264,2048]{1,0:T(8,128)(2,1)S(1)} %shard_map.38.middle_ref), channel_id=1, source_target_pairs={{4,8},{12,16},{20,24},{8,4},{16,12},{24,20},{5,9},{13,17},{21,25},... | collective-permute-start | bytes 3244040 | tf_op jit(solution)/shard_map/ppermute | solution.py:239
  13.0 5.7 %collective-permute-start.3 = (bf16[520,2048]{1,0:T(8,128)(2,1)S(1)}, bf16[520,2048]{1,0:T(8,128)(2,1)S(1)}, u32[]{:S(2)}, u32[]{:S(2)}) collective-permute-start(bf16[520,2048]{1,0:T(8,128)(2,1)S(1)} %get-tuple-element.18.whole_ref), channel_id=1, source_target_pairs={{0,4},{4,0},{8,12},{12,8},{16,20},{20,16},{24,28},{28,24},{1,5},{5... | collective-permute-start | bytes 6389768 | tf_op jit(solution)/shard_map/ppermute | solution.py:250
  13.0 9.9 %collective-permute-start.1 = (bf16[128,2048]{1,0:T(8,128)(2,1)S(1)}, bf16[128,2048]{1,0:T(8,128)(2,1)S(1)}, u32[]{:S(2)}, u32[]{:S(2)}) collective-permute-start(bf16[128,2048]{1,0:T(8,128)(2,1)S(1)} %collective-permute-done.direct_ref), channel_id=1, source_target_pairs={{4,6},{5,7},{6,4},{7,5},{8,9},{9,8},{10,11},{11,10},{12,14},{13,15... | collective-permute-start | bytes 1572872 | tf_op jit(solution)/shard_map/ppermute | solution.py:251
  21.2 3.4 %collective-permute-start.4 = (f32[1,512]{1,0:T(1,128)S(1)}, f32[1,512]{1,0:T(1,128)S(1)}, u32[]{:S(2)}, u32[]{:S(2)}) collective-permute-start(f32[1,512]{1,0:T(1,128)S(1)} %shard_map.41), channel_id=1, source_target_pairs={{0,4},{4,0},{8,12},{12,8},{16,20},{20,16},{24,28},{28,24},{1,5},{5... | collective-permute-start | bytes 6152 | tf_op jit(solution)/shard_map/ppermute | solution.py:254

commit v5 on v3

--- a/solution.py
+++ b/solution.py
@@ -54,6 +54,12 @@
     index = lax.broadcasted_iota(jnp.int32, score.shape, 0)
     inside = (index >= bounds[0] - first) & (index <= bounds[1] - first)
     return jnp.max(jnp.where(inside, score, LOWEST), axis=0, keepdims=True)
+
+
+def meets(bounds, peptides_ref):
+    first = place(peptides_ref)[0]
+    inside = (bounds[0] < first + peptides_ref.shape[0]) & (bounds[1] >= first)
+    return jnp.max(inside.astype(jnp.int32)) > 0
 
 
 def write_note(note_ref, bounds_ref):
@@ -158,19 +164,22 @@
         count = rows - 2 * part
         bounds = read_note(middle_ref.at[count:], rows)
         first = place(peptides_ref)[0]
-        far_best[:, part : part + count] = best_of(
-            middle_ref[:count, :],
-            peptides_ref[...],
-            [bound[:, part : part + count] for bound in bounds],
-            first,
-        )
+        inside = [bound[:, part : part + count] for bound in bounds]
         ends = [
             jnp.concatenate([bound[:, :part], bound[:, part + count :]], axis=1)
             for bound in bounds
         ]
+
+        needed = meets(inside, peptides_ref)
         best = best_of(outer[...], peptides_ref[...], ends, first)
         far_best[:, :part] = best[:, :part]
         far_best[:, part + count :] = best[:, part:]
+
+        @pl.when(needed)
+        def _():
+            far_best[:, part : part + count] = best_of(
+                middle_ref[:count, :], peptides_ref[...], inside, first
+            )
 
     near = jnp.maximum(own_ref[...], back_ref[...])
     half = (out_ref.shape[0] // 2, rows)

time: 38.2 us -> 37.3 us (0.976)
  Pallas kernels: 13.7 us -> 12.4 us
    pallas_call x1, Pallas kernels: 2.62 us -> 1.4 us  [per_device(): call(last_kernel, [((2 * shards, rows), f32)], [VMEM] * 6, [pltpu.VMEM((2...]
  transfers between devices with their start and end apart: 5 -> 5, of which waited for: 3 -> 3; matrix products, arithmetic and copies ran while one was open for 0% -> 0% of each run, Pallas kernels for 25% -> 26%
where the time goes in v5:
time: 37.3 us; the launch traced here: 37.1 us
  Pallas kernels  12.4 us (33%)
  blocking collectives  10 us (27%)
  starting transfers between devices  9.73 us (26%)
  waiting for transfers between devices  4.16 us (11%)
  other arithmetic  0.61 us (2%)
    all_to_all x1, blocking collectives, per_device(): lax.all_to_all(bests, ('mass', 'pep'), 0, 0, axis_index_groups=groups)  10 us
    ppermute x1, starting transfers between devices, per_device(): direct = lax.ppermute(quarter, 'mass', across)  4.59 us
    ppermute x1, starting transfers between devices, per_device(): relayed = lax.ppermute(direct, ('mass', 'pep'), relay)  3.14 us
    pallas_call x1, Pallas kernels, per_device(): near_best, = call(near_kernel, *score)(near, held)  2.54 us
    pallas_call x1, Pallas kernels, per_device(): own_best, = call(near_kernel, *score, LONG)(whole, held)  2.54 us
    pallas_call x1, Pallas kernels, per_device(): call(whole_kernel, [((rows + NOTE, bins), bf16), (peptides.shape, bf16)],...  2.4 us
    ppermute x1, waiting for transfers between devices, per_device(): far = lax.ppermute(middle, 'mass', across)  2.09 us
    pallas_call x1, Pallas kernels, per_device(): call(middle_kernel, [((rows - 2 * part + NOTE, bins), bf16)], [HBM, HBM],...  2.03 us
  transfers between devices with their start and end apart: 5, of which 3 were waited for; matrix products, arithmetic and copies ran while one was open for 0% of the time, Pallas kernels for 26%

profile of v5, /device:TPU:1, one launch (start us, length us, event | category | flops | bytes accessed | tf_op | source)
XLA Modules:
  0.0 37.1 jit_solution(6571774257854369322)
XLA Ops:
  0.0 1.5 %shard_map.37.quarter_ref = bf16[128,2048]{1,0:T(8,128)(2,1)S(1)} custom-call(bf16[512,2048]{1,0:T(8,128)(2,1)} %spectra_ref.5), custom_call_target="tpu_custom_call" | custom-call | flops 1024 | bytes 1024 | tf_op jit(solution)/shard_map/pallas_call | solution.py:229
  1.5 4.6 %collective-permute-start = (bf16[128,2048]{1,0:T(8,128)(2,1)S(1)}, bf16[128,2048]{1,0:T(8,128)(2,1)S(1)}, u32[]{:S(2)}, u32[]{:S(2)}) collective-permute-start(bf16[128,2048]{1,0:T(8,128)(2,1)S(1)} %shard_map.37.quarter_ref), channel_id=1, source_target_pairs={{4,8},{12,16},{20,24},{8,4},{16,12},{24,20},{5,9},{13,17},{21,25},... | collective-permute-start | bytes 1572872 | tf_op jit(solution)/shard_map/ppermute | solution.py:235
  6.1 2.0 %shard_map.38.middle_ref = bf16[272,2048]{1,0:T(8,128)(2,1)S(1)} custom-call(bf16[512,2048]{1,0:T(8,128)(2,1)} %spectra_ref.5, s32[2,512]{1,0:T(2,128)} %bitcast.3), custom_call_target="tpu_custom_call" | custom-call | flops 1024 | bytes 1024 | tf_op jit(solution)/shard_map/pallas_call | solution.py:238
  8.2 1.9 %collective-permute-start.2 = (bf16[272,2048]{1,0:T(8,128)(2,1)S(1)}, bf16[272,2048]{1,0:T(8,128)(2,1)S(1)}, u32[]{:S(2)}, u32[]{:S(2)}) collective-permute-start(bf16[272,2048]{1,0:T(8,128)(2,1)S(1)} %shard_map.38.middle_ref), channel_id=1, source_target_pairs={{4,8},{12,16},{20,24},{8,4},{16,12},{24,20},{5,9},{13,17},{21,25},... | collective-permute-start | bytes 3342344 | tf_op jit(solution)/shard_map/ppermute | solution.py:248
  10.1 2.4 %shard_map.39 = (bf16[528,2048]{1,0:T(8,128)(2,1)S(1)}, bf16[1024,2048]{1,0:T(8,128)(2,1)S(1)}) custom-call(bf16[512,2048]{1,0:T(8,128)(2,1)} %spectra_ref.5, bf16[1024,2048]{1,0:T(8,128)(2,1)} %peptides_ref.1, bf16[128,2048]{1,0:T(8,128)(2,1)S(1)} %shard_map.37.quarter_ref, bf16[272,2048]{1,0:T(8,128)(2,1)S(1)} %shard_map.38.middle_ref), custom_call_target="tpu_custom_call" | custom-call | flops 1024 | bytes 1024 | tf_op jit(solution)/shard_map/pallas_call | solution.py:249
  12.5 0.5 %collective-permute-done.direct_ref = bf16[128,2048]{1,0:T(8,128)(2,1)S(1)} collective-permute-done((bf16[128,2048]{1,0:T(8,128)(2,1)S(1)}, bf16[128,2048]{1,0:T(8,128)(2,1)S(1)}, u32[]{:S(2)}, u32[]{:S(2)}) %collective-permute-start) | collective-permute-done | bytes 524320 | tf_op jit(solution)/shard_map/ppermute | solution.py:235
  13.0 0.0 collective-permute-start.3
  13.0 3.1 %collective-permute-start.1 = (bf16[128,2048]{1,0:T(8,128)(2,1)S(1)}, bf16[128,2048]{1,0:T(8,128)(2,1)S(1)}, u32[]{:S(2)}, u32[]{:S(2)}) collective-permute-start(bf16[128,2048]{1,0:T(8,128)(2,1)S(1)} %collective-permute-done.direct_ref), channel_id=1, source_target_pairs={{4,6},{5,7},{6,4},{7,5},{8,9},{9,8},{10,11},{11,10},{12,14},{13,15... | collective-permute-start | bytes 1572872 | tf_op jit(solution)/shard_map/ppermute | solution.py:260
  16.1 2.5 %shard_map.40.own_ref = f32[1,512]{1,0:T(1,128)S(1)} custom-call(bf16[528,2048]{1,0:T(8,128)(2,1)S(1)} %get-tuple-element.18.whole_ref, bf16[1024,2048]{1,0:T(8,128)(2,1)S(1)} %get-tuple-element.17.peptides_ref), custom_call_target="tpu_custom_call" | custom-call | flops 34359738368 | bytes 1024 | tf_op jit(solution)/shard_map/pallas_call | solution.py:257
  18.7 0.0 collective-permute-done.3.whole_ref
  18.7 2.5 %shard_map.41 = f32[1,512]{1,0:T(1,128)S(1)} custom-call(bf16[528,2048]{1,0:T(8,128)(2,1)S(1)} %collective-permute-done.3.whole_ref, bf16[1024,2048]{1,0:T(8,128)(2,1)S(1)} %get-tuple-element.17.peptides_ref), custom_call_target="tpu_custom_call" | custom-call | flops 1024 | bytes 1024 | tf_op jit(solution)/shard_map/pallas_call | solution.py:262
  21.2 0.1 collective-permute-start.4
  21.3 1.6 %collective-permute-done.1.relayed_ref = bf16[128,2048]{1,0:T(8,128)(2,1)S(1)} collective-permute-done((bf16[128,2048]{1,0:T(8,128)(2,1)S(1)}, bf16[128,2048]{1,0:T(8,128)(2,1)S(1)}, u32[]{:S(2)}, u32[]{:S(2)}) %collective-permute-start.1) | collective-permute-done | bytes 524320 | tf_op jit(solution)/shard_map/ppermute | solution.py:260
  22.9 2.1 %collective-permute-done.2.middle_ref = bf16[272,2048]{1,0:T(8,128)(2,1)S(1)} collective-permute-done((bf16[272,2048]{1,0:T(8,128)(2,1)S(1)}, bf16[272,2048]{1,0:T(8,128)(2,1)S(1)}, u32[]{:S(2)}, u32[]{:S(2)}) %collective-permute-start.2) | collective-permute-done | bytes 1114144 | tf_op jit(solution)/shard_map/ppermute | solution.py:248
  25.0 0.0 collective-permute-done.4.back_ref
  25.0 1.4 %shard_map.42 = f32[8,512]{1,0:T(8,128)S(1)} custom-call(bf16[128,2048]{1,0:T(8,128)(2,1)S(1)} %collective-permute-done.direct_ref, bf16[128,2048]{1,0:T(8,128)(2,1)S(1)} %collective-permute-done.1.relayed_ref, bf16[272,2048]{1,0:T(8,128)(2,1)S(1)} %collective-permute-done.2.middle_ref, bf16[1024,2048]{1,0:T(8,128)(2,1)S(1)} %get-tuple-element.17.peptides_ref, ...), custom_call_target="tpu_custom_call" | custom-call | flops 1024 | bytes 1024 | tf_op jit(solution)/shard_map/pallas_call | solution.py:265
  26.4 10.0 %all_to_all.9 = f32[8,1,512]{2,1,0:T(1,128)S(1)} all-to-all(f32[8,1,512]{2,1,0:T(1,128)S(1)} %copy.4), channel_id=1, replica_groups={{4,5,6,7,8,9,10,11},{12,13,14,15,16,17,18,19},{20,21,22,23,24,25,26,27}..., dimensions={0} | all-to-all | bytes 32768 | tf_op jit(solution)/shard_map/all_to_all | solution.py:271
  36.5 0.6 %reduce_max.9 = f32[512]{0:T(512)} reduce(f32[8,1,512]{2,1,0:T(1,128)S(1)} %all_to_all.9, f32[]{:T(128)} %constant.0.clone.1), dimensions={0,1}, to_apply=%region_0.0 | reduce | flops 3584 | bytes 18436 | tf_op jit(solution)/shard_map/reduce_max | solution.py:272
  (1 shorter events, 0.0 us)
Async XLA Ops:
  1.5 11.5 %collective-permute-start = (bf16[128,2048]{1,0:T(8,128)(2,1)S(1)}, bf16[128,2048]{1,0:T(8,128)(2,1)S(1)}, u32[]{:S(2)}, u32[]{:S(2)}) collective-permute-start(bf16[128,2048]{1,0:T(8,128)(2,1)S(1)} %shard_map.37.quarter_ref), channel_id=1, source_target_pairs={{4,8},{12,16},{20,24},{8,4},{16,12},{24,20},{5,9},{13,17},{21,25},... | collective-permute-start | bytes 1572872 | tf_op jit(solution)/shard_map/ppermute | solution.py:235
  8.2 16.8 %collective-permute-start.2 = (bf16[272,2048]{1,0:T(8,128)(2,1)S(1)}, bf16[272,2048]{1,0:T(8,128)(2,1)S(1)}, u32[]{:S(2)}, u32[]{:S(2)}) collective-permute-start(bf16[272,2048]{1,0:T(8,128)(2,1)S(1)} %shard_map.38.middle_ref), channel_id=1, source_target_pairs={{4,8},{12,16},{20,24},{8,4},{16,12},{24,20},{5,9},{13,17},{21,25},... | collective-permute-start | bytes 3342344 | tf_op jit(solution)/shard_map/ppermute | solution.py:248
  13.0 5.7 %collective-permute-start.3 = (bf16[528,2048]{1,0:T(8,128)(2,1)S(1)}, bf16[528,2048]{1,0:T(8,128)(2,1)S(1)}, u32[]{:S(2)}, u32[]{:S(2)}) collective-permute-start(bf16[528,2048]{1,0:T(8,128)(2,1)S(1)} %get-tuple-element.18.whole_ref), channel_id=1, source_target_pairs={{0,4},{4,0},{8,12},{12,8},{16,20},{20,16},{24,28},{28,24},{1,5},{5... | collective-permute-start | bytes 6488072 | tf_op jit(solution)/shard_map/ppermute | solution.py:259
  13.0 9.9 %collective-permute-start.1 = (bf16[128,2048]{1,0:T(8,128)(2,1)S(1)}, bf16[128,2048]{1,0:T(8,128)(2,1)S(1)}, u32[]{:S(2)}, u32[]{:S(2)}) collective-permute-start(bf16[128,2048]{1,0:T(8,128)(2,1)S(1)} %collective-permute-done.direct_ref), channel_id=1, source_target_pairs={{4,6},{5,7},{6,4},{7,5},{8,9},{9,8},{10,11},{11,10},{12,14},{13,15... | collective-permute-start | bytes 1572872 | tf_op jit(solution)/shard_map/ppermute | solution.py:260
  21.2 3.8 %collective-permute-start.4 = (f32[1,512]{1,0:T(1,128)S(1)}, f32[1,512]{1,0:T(1,128)S(1)}, u32[]{:S(2)}, u32[]{:S(2)}) collective-permute-start(f32[1,512]{1,0:T(1,128)S(1)} %shard_map.41), channel_id=1, source_target_pairs={{0,4},{4,0},{8,12},{12,8},{16,20},{20,16},{24,28},{28,24},{1,5},{5... | collective-permute-start | bytes 6152 | tf_op jit(solution)/shard_map/ppermute | solution.py:263

commit v6 on v5

--- a/solution.py
+++ b/solution.py
@@ -12,7 +12,7 @@
 HBM = pl.BlockSpec(memory_space=pltpu.HBM)
 BLOCK = 256
 PAD = 128
-NOTE = 16
+NOTE = 8
 LONG = 2**35
 DIGITS = 3
 
@@ -255,7 +255,6 @@
 
     score = [((1, rows), f32)], [VMEM, VMEM], []
     (own_best,) = call(near_kernel, *score, LONG)(whole, held)
-    direct, whole = lax.optimization_barrier((direct, whole))
     near = lax.ppermute(whole, "mass", chip)
     relayed = lax.ppermute(direct, ("mass", "pep"), relay)
     near, own_best = lax.optimization_barrier((near, own_best))

time: 37.3 us -> 37 us (level)
  waiting for transfers between devices: 4.16 us -> 3.73 us
where the time goes in v6:
time: 37 us; the launch traced here: 36.7 us
  Pallas kernels  12.4 us (34%)
  blocking collectives  10 us (27%)
  starting transfers between devices  9.79 us (26%)
  waiting for transfers between devices  3.73 us (10%)
  other arithmetic  0.61 us (2%)
    all_to_all x1, blocking collectives, per_device(): lax.all_to_all(bests, ('mass', 'pep'), 0, 0, axis_index_groups=groups)  10 us
    ppermute x1, starting transfers between devices, per_device(): direct = lax.ppermute(quarter, 'mass', across)  4.59 us
    ppermute x1, starting transfers between devices, per_device(): relayed = lax.ppermute(direct, ('mass', 'pep'), relay)  3.14 us
    pallas_call x1, Pallas kernels, per_device(): own_best, = call(near_kernel, *score, LONG)(whole, held)  2.55 us
    pallas_call x1, Pallas kernels, per_device(): near_best, = call(near_kernel, *score)(near, held)  2.54 us
    pallas_call x1, Pallas kernels, per_device(): call(whole_kernel, [((rows + NOTE, bins), bf16), (peptides.shape, bf16)],...  2.4 us
    pallas_call x1, Pallas kernels, per_device(): call(middle_kernel, [((rows - 2 * part + NOTE, bins), bf16)], [HBM, HBM],...  2.03 us
    ppermute x1, starting transfers between devices, per_device(): far = lax.ppermute(middle, 'mass', across)  1.92 us
  transfers between devices with their start and end apart: 5, of which 3 were waited for; matrix products, arithmetic and copies ran while one was open for 0% of the time, Pallas kernels for 26%

profile of v6, /device:TPU:1, one launch (start us, length us, event | category | flops | bytes accessed | tf_op | source)
XLA Modules:
  0.0 36.7 jit_solution(17503998471919135632)
XLA Ops:
  0.0 1.5 %shard_map.37.quarter_ref = bf16[128,2048]{1,0:T(8,128)(2,1)S(1)} custom-call(bf16[512,2048]{1,0:T(8,128)(2,1)} %spectra_ref.5), custom_call_target="tpu_custom_call" | custom-call | flops 1024 | bytes 1024 | tf_op jit(solution)/shard_map/pallas_call | solution.py:229
  1.5 4.6 %collective-permute-start = (bf16[128,2048]{1,0:T(8,128)(2,1)S(1)}, bf16[128,2048]{1,0:T(8,128)(2,1)S(1)}, u32[]{:S(2)}, u32[]{:S(2)}) collective-permute-start(bf16[128,2048]{1,0:T(8,128)(2,1)S(1)} %shard_map.37.quarter_ref), channel_id=1, source_target_pairs={{4,8},{12,16},{20,24},{8,4},{16,12},{24,20},{5,9},{13,17},{21,25},... | collective-permute-start | bytes 1572872 | tf_op jit(solution)/shard_map/ppermute | solution.py:235
  6.1 2.0 %shard_map.38.middle_ref = bf16[264,2048]{1,0:T(8,128)(2,1)S(1)} custom-call(bf16[512,2048]{1,0:T(8,128)(2,1)} %spectra_ref.5, s32[2,512]{1,0:T(2,128)} %bitcast.3), custom_call_target="tpu_custom_call" | custom-call | flops 1024 | bytes 1024 | tf_op jit(solution)/shard_map/pallas_call | solution.py:238
  8.2 1.9 %collective-permute-start.2 = (bf16[264,2048]{1,0:T(8,128)(2,1)S(1)}, bf16[264,2048]{1,0:T(8,128)(2,1)S(1)}, u32[]{:S(2)}, u32[]{:S(2)}) collective-permute-start(bf16[264,2048]{1,0:T(8,128)(2,1)S(1)} %shard_map.38.middle_ref), channel_id=1, source_target_pairs={{4,8},{12,16},{20,24},{8,4},{16,12},{24,20},{5,9},{13,17},{21,25},... | collective-permute-start | bytes 3244040 | tf_op jit(solution)/shard_map/ppermute | solution.py:248
  10.1 2.4 %shard_map.39 = (bf16[520,2048]{1,0:T(8,128)(2,1)S(1)}, bf16[1024,2048]{1,0:T(8,128)(2,1)S(1)}) custom-call(bf16[512,2048]{1,0:T(8,128)(2,1)} %spectra_ref.5, bf16[1024,2048]{1,0:T(8,128)(2,1)} %peptides_ref.1, bf16[128,2048]{1,0:T(8,128)(2,1)S(1)} %shard_map.37.quarter_ref, bf16[264,2048]{1,0:T(8,128)(2,1)S(1)} %shard_map.38.middle_ref), custom_call_target="tpu_custom_call" | custom-call | flops 1024 | bytes 1024 | tf_op jit(solution)/shard_map/pallas_call | solution.py:249
  12.5 0.1 collective-permute-start.3
  12.6 0.4 %collective-permute-done.direct_ref = bf16[128,2048]{1,0:T(8,128)(2,1)S(1)} collective-permute-done((bf16[128,2048]{1,0:T(8,128)(2,1)S(1)}, bf16[128,2048]{1,0:T(8,128)(2,1)S(1)}, u32[]{:S(2)}, u32[]{:S(2)}) %collective-permute-start) | collective-permute-done | bytes 524320 | tf_op jit(solution)/shard_map/ppermute | solution.py:235
  13.0 3.1 %collective-permute-start.1 = (bf16[128,2048]{1,0:T(8,128)(2,1)S(1)}, bf16[128,2048]{1,0:T(8,128)(2,1)S(1)}, u32[]{:S(2)}, u32[]{:S(2)}) collective-permute-start(bf16[128,2048]{1,0:T(8,128)(2,1)S(1)} %collective-permute-done.direct_ref), channel_id=1, source_target_pairs={{4,6},{5,7},{6,4},{7,5},{8,9},{9,8},{10,11},{11,10},{12,14},{13,15... | collective-permute-start | bytes 1572872 | tf_op jit(solution)/shard_map/ppermute | solution.py:259
  16.1 2.5 %shard_map.40.own_ref = f32[1,512]{1,0:T(1,128)S(1)} custom-call(bf16[520,2048]{1,0:T(8,128)(2,1)S(1)} %get-tuple-element.14.whole_ref, bf16[1024,2048]{1,0:T(8,128)(2,1)S(1)} %get-tuple-element.13.peptides_ref), custom_call_target="tpu_custom_call" | custom-call | flops 34359738368 | bytes 1024 | tf_op jit(solution)/shard_map/pallas_call | solution.py:257
  18.7 0.0 collective-permute-done.3.whole_ref
  18.7 2.5 %shard_map.41 = f32[1,512]{1,0:T(1,128)S(1)} custom-call(bf16[520,2048]{1,0:T(8,128)(2,1)S(1)} %collective-permute-done.3.whole_ref, bf16[1024,2048]{1,0:T(8,128)(2,1)S(1)} %get-tuple-element.13.peptides_ref), custom_call_target="tpu_custom_call" | custom-call | flops 1024 | bytes 1024 | tf_op jit(solution)/shard_map/pallas_call | solution.py:261
  21.2 0.1 collective-permute-start.4
  21.3 1.6 %collective-permute-done.1.relayed_ref = bf16[128,2048]{1,0:T(8,128)(2,1)S(1)} collective-permute-done((bf16[128,2048]{1,0:T(8,128)(2,1)S(1)}, bf16[128,2048]{1,0:T(8,128)(2,1)S(1)}, u32[]{:S(2)}, u32[]{:S(2)}) %collective-permute-start.1) | collective-permute-done | bytes 524320 | tf_op jit(solution)/shard_map/ppermute | solution.py:259
  22.9 1.7 %collective-permute-done.2.middle_ref = bf16[264,2048]{1,0:T(8,128)(2,1)S(1)} collective-permute-done((bf16[264,2048]{1,0:T(8,128)(2,1)S(1)}, bf16[264,2048]{1,0:T(8,128)(2,1)S(1)}, u32[]{:S(2)}, u32[]{:S(2)}) %collective-permute-start.2) | collective-permute-done | bytes 1081376 | tf_op jit(solution)/shard_map/ppermute | solution.py:248
  24.7 0.0 collective-permute-done.4.back_ref
  24.7 1.4 %shard_map.42 = f32[8,512]{1,0:T(8,128)S(1)} custom-call(bf16[128,2048]{1,0:T(8,128)(2,1)S(1)} %collective-permute-done.direct_ref, bf16[128,2048]{1,0:T(8,128)(2,1)S(1)} %collective-permute-done.1.relayed_ref, bf16[264,2048]{1,0:T(8,128)(2,1)S(1)} %collective-permute-done.2.middle_ref, bf16[1024,2048]{1,0:T(8,128)(2,1)S(1)} %get-tuple-element.13.peptides_ref, ...), custom_call_target="tpu_custom_call" | custom-call | flops 1024 | bytes 1024 | tf_op jit(solution)/shard_map/pallas_call | solution.py:264
  26.1 10.0 %all_to_all.9 = f32[8,1,512]{2,1,0:T(1,128)S(1)} all-to-all(f32[8,1,512]{2,1,0:T(1,128)S(1)} %copy.4), channel_id=1, replica_groups={{4,5,6,7,8,9,10,11},{12,13,14,15,16,17,18,19},{20,21,22,23,24,25,26,27}..., dimensions={0} | all-to-all | bytes 32768 | tf_op jit(solution)/shard_map/all_to_all | solution.py:270
  36.1 0.6 %reduce_max.9 = f32[512]{0:T(512)} reduce(f32[8,1,512]{2,1,0:T(1,128)S(1)} %all_to_all.9, f32[]{:T(128)} %constant.0.clone.1), dimensions={0,1}, to_apply=%region_0.0 | reduce | flops 3584 | bytes 18436 | tf_op jit(solution)/shard_map/reduce_max | solution.py:271
  (1 shorter events, 0.0 us)
Async XLA Ops:
  1.5 11.5 %collective-permute-start = (bf16[128,2048]{1,0:T(8,128)(2,1)S(1)}, bf16[128,2048]{1,0:T(8,128)(2,1)S(1)}, u32[]{:S(2)}, u32[]{:S(2)}) collective-permute-start(bf16[128,2048]{1,0:T(8,128)(2,1)S(1)} %shard_map.37.quarter_ref), channel_id=1, source_target_pairs={{4,8},{12,16},{20,24},{8,4},{16,12},{24,20},{5,9},{13,17},{21,25},... | collective-permute-start | bytes 1572872 | tf_op jit(solution)/shard_map/ppermute | solution.py:235
  8.2 16.5 %collective-permute-start.2 = (bf16[264,2048]{1,0:T(8,128)(2,1)S(1)}, bf16[264,2048]{1,0:T(8,128)(2,1)S(1)}, u32[]{:S(2)}, u32[]{:S(2)}) collective-permute-start(bf16[264,2048]{1,0:T(8,128)(2,1)S(1)} %shard_map.38.middle_ref), channel_id=1, source_target_pairs={{4,8},{12,16},{20,24},{8,4},{16,12},{24,20},{5,9},{13,17},{21,25},... | collective-permute-start | bytes 3244040 | tf_op jit(solution)/shard_map/ppermute | solution.py:248
  12.5 6.2 %collective-permute-start.3 = (bf16[520,2048]{1,0:T(8,128)(2,1)S(1)}, bf16[520,2048]{1,0:T(8,128)(2,1)S(1)}, u32[]{:S(2)}, u32[]{:S(2)}) collective-permute-start(bf16[520,2048]{1,0:T(8,128)(2,1)S(1)} %get-tuple-element.14.whole_ref), channel_id=1, source_target_pairs={{0,4},{4,0},{8,12},{12,8},{16,20},{20,16},{24,28},{28,24},{1,5},{5... | collective-permute-start | bytes 6389768 | tf_op jit(solution)/shard_map/ppermute | solution.py:258
  13.0 9.9 %collective-permute-start.1 = (bf16[128,2048]{1,0:T(8,128)(2,1)S(1)}, bf16[128,2048]{1,0:T(8,128)(2,1)S(1)}, u32[]{:S(2)}, u32[]{:S(2)}) collective-permute-start(bf16[128,2048]{1,0:T(8,128)(2,1)S(1)} %collective-permute-done.direct_ref), channel_id=1, source_target_pairs={{4,6},{5,7},{6,4},{7,5},{8,9},{9,8},{10,11},{11,10},{12,14},{13,15... | collective-permute-start | bytes 1572872 | tf_op jit(solution)/shard_map/ppermute | solution.py:259
  21.2 3.4 %collective-permute-start.4 = (f32[1,512]{1,0:T(1,128)S(1)}, f32[1,512]{1,0:T(1,128)S(1)}, u32[]{:S(2)}, u32[]{:S(2)}) collective-permute-start(f32[1,512]{1,0:T(1,128)S(1)} %shard_map.41), channel_id=1, source_target_pairs={{0,4},{4,0},{8,12},{12,8},{16,20},{20,16},{24,28},{28,24},{1,5},{5... | collective-permute-start | bytes 6152 | tf_op jit(solution)/shard_map/ppermute | solution.py:262

commit v7 on v6

--- a/solution.py
+++ b/solution.py
@@ -82,7 +82,7 @@
     ]
 
 
-def quarter_kernel(spectra_ref, quarter_ref, raw, sems):
+def quarter_kernel(spectra_ref, quarter_ref, sems):
     part = quarter_ref.shape[0]
     start = place(spectra_ref)[3] * (spectra_ref.shape[0] - part)
     step = part // sems.shape[0]
@@ -90,7 +90,7 @@
     copies = [
         pltpu.make_async_copy(
             spectra_ref.at[pl.ds(pl.multiple_of(start + low, 16), size)],
-            raw.at[low : low + size],
+            quarter_ref.at[low : low + size],
             sems.at[i],
         )
         for i, (low, size) in enumerate(cuts)
@@ -99,7 +99,10 @@
         copy.start()
     for copy in copies:
         copy.wait()
-    process_into(raw, quarter_ref)
+
+
+def process_kernel(rows_ref, processed_ref):
+    process_into(rows_ref, processed_ref)
 
 
 def middle_kernel(spectra_ref, bounds_ref, middle_ref, raw, windows, sems):
@@ -127,7 +130,7 @@
     peptides = pltpu.make_async_copy(peptides_ref, held_ref, sems.at[1])
     rest.start()
     peptides.start()
-    whole_ref[pl.ds(start, part), :] = quarter_ref[...]
+    process_into(quarter_ref, whole_ref.at[pl.ds(start, part)])
     whole_ref[part : rows - part, :] = middle_ref[: rows - 2 * part, :]
     whole_ref[rows:, :] = middle_ref[rows - 2 * part :, :]
     rest.wait()
@@ -230,7 +233,7 @@
         quarter_kernel,
         [((part, bins), bf16)],
         [HBM],
-        [pltpu.VMEM((part, bins), bf16), pltpu.SemaphoreType.DMA((2,))],
+        [pltpu.SemaphoreType.DMA((2,))],
     )(spectra)
     direct = lax.ppermute(quarter, "mass", across)
 
@@ -257,9 +260,13 @@
     (own_best,) = call(near_kernel, *score, LONG)(whole, held)
     near = lax.ppermute(whole, "mass", chip)
     relayed = lax.ppermute(direct, ("mass", "pep"), relay)
-    near, own_best = lax.optimization_barrier((near, own_best))
+    (direct,) = call(process_kernel, [((part, bins), bf16)], [VMEM], [])(direct)
+    near, own_best, direct = lax.optimization_barrier((near, own_best, direct))
     (near_best,) = call(near_kernel, *score)(near, held)
     back = lax.ppermute(near_best, "mass", chip)
+    relayed, near_best = lax.optimization_barrier((relayed, near_best))
+    (relayed,) = call(process_kernel, [((part, bins), bf16)], [VMEM], [])(relayed)
+    far, relayed = lax.optimization_barrier((far, relayed))
 
     (bests,) = call(
         last_kernel,

time: 37 us -> 36.5 us (0.986)
  waiting for transfers between devices: 3.73 us -> 2.71 us
  Pallas kernels: 12.4 us -> 12.9 us
    pallas_call x1 -> x3, Pallas kernels: 1.53 us -> 2.05 us  [the longest x1 1.04 us: per_device(): call(quarter_kernel, [((part, bins), bf16)], [HBM], [pltpu.SemaphoreType....]
    ppermute x1, waiting for transfers between devices: 1.75 us -> 1.24 us  [per_device(): far = lax.ppermute(middle, 'mass', across)]
    ppermute x1, waiting for transfers between devices: 1.58 us -> 1.08 us  [per_device(): relayed = lax.ppermute(direct, ('mass', 'pep'), relay)]
  transfers between devices with their start and end apart: 5 -> 5, of which waited for: 3 -> 3; matrix products, arithmetic and copies ran while one was open for 0% -> 0% of each run, Pallas kernels for 26% -> 29%
where the time goes in v7:
time: 36.5 us; the launch traced here: 36.2 us
  Pallas kernels  12.9 us (35%)
  blocking collectives  10 us (27%)
  starting transfers between devices  9.79 us (27%)
  waiting for transfers between devices  2.71 us (7%)
  other arithmetic  0.61 us (2%)
    all_to_all x1, blocking collectives, per_device(): lax.all_to_all(bests, ('mass', 'pep'), 0, 0, axis_index_groups=groups)  10 us
    ppermute x1, starting transfers between devices, per_device(): direct = lax.ppermute(quarter, 'mass', across)  4.59 us
    ppermute x1, starting transfers between devices, per_device(): relayed = lax.ppermute(direct, ('mass', 'pep'), relay)  3.14 us
    pallas_call x1, Pallas kernels, per_device(): own_best, = call(near_kernel, *score, LONG)(whole, held)  2.54 us
    pallas_call x1, Pallas kernels, per_device(): near_best, = call(near_kernel, *score)(near, held)  2.54 us
    pallas_call x1, Pallas kernels, per_device(): call(whole_kernel, [((rows + NOTE, bins), bf16), (peptides.shape, bf16)],...  2.4 us
    pallas_call x1, Pallas kernels, per_device(): call(middle_kernel, [((rows - 2 * part + NOTE, bins), bf16)], [HBM, HBM],...  2.03 us
    ppermute x1, starting transfers between devices, per_device(): far = lax.ppermute(middle, 'mass', across)  1.92 us
  transfers between devices with their start and end apart: 5, of which 3 were waited for; matrix products, arithmetic and copies ran while one was open for 0% of the time, Pallas kernels for 29%

profile of v7, /device:TPU:1, one launch (start us, length us, event | category | flops | bytes accessed | tf_op | source)
XLA Modules:
  0.0 36.2 jit_solution(4600729957324741725)
XLA Ops:
  0.0 1.0 %shard_map.37.quarter_ref = bf16[128,2048]{1,0:T(8,128)(2,1)S(1)} custom-call(bf16[512,2048]{1,0:T(8,128)(2,1)} %spectra_ref.5), custom_call_target="tpu_custom_call" | custom-call | flops 1024 | bytes 1024 | tf_op jit(solution)/shard_map/pallas_call | solution.py:232
  1.1 4.6 %collective-permute-start.1 = (bf16[128,2048]{1,0:T(8,128)(2,1)S(1)}, bf16[128,2048]{1,0:T(8,128)(2,1)S(1)}, u32[]{:S(2)}, u32[]{:S(2)}) collective-permute-start(bf16[128,2048]{1,0:T(8,128)(2,1)S(1)} %shard_map.37.quarter_ref), channel_id=1, source_target_pairs={{4,8},{12,16},{20,24},{8,4},{16,12},{24,20},{5,9},{13,17},{21,25},... | collective-permute-start | bytes 1572872 | tf_op jit(solution)/shard_map/ppermute | solution.py:238
  5.7 2.0 %shard_map.38.middle_ref = bf16[264,2048]{1,0:T(8,128)(2,1)S(1)} custom-call(bf16[512,2048]{1,0:T(8,128)(2,1)} %spectra_ref.5, s32[2,512]{1,0:T(2,128)} %bitcast.3), custom_call_target="tpu_custom_call" | custom-call | flops 1024 | bytes 1024 | tf_op jit(solution)/shard_map/pallas_call | solution.py:241
  7.7 1.9 %collective-permute-start.2 = (bf16[264,2048]{1,0:T(8,128)(2,1)S(1)}, bf16[264,2048]{1,0:T(8,128)(2,1)S(1)}, u32[]{:S(2)}, u32[]{:S(2)}) collective-permute-start(bf16[264,2048]{1,0:T(8,128)(2,1)S(1)} %shard_map.38.middle_ref), channel_id=1, source_target_pairs={{4,8},{12,16},{20,24},{8,4},{16,12},{24,20},{5,9},{13,17},{21,25},... | collective-permute-start | bytes 3244040 | tf_op jit(solution)/shard_map/ppermute | solution.py:251
  9.6 2.4 %shard_map.39 = (bf16[520,2048]{1,0:T(8,128)(2,1)S(1)}, bf16[1024,2048]{1,0:T(8,128)(2,1)S(1)}) custom-call(bf16[512,2048]{1,0:T(8,128)(2,1)} %spectra_ref.5, bf16[1024,2048]{1,0:T(8,128)(2,1)} %peptides_ref.1, bf16[128,2048]{1,0:T(8,128)(2,1)S(1)} %shard_map.37.quarter_ref, bf16[264,2048]{1,0:T(8,128)(2,1)S(1)} %shard_map.38.middle_ref), custom_call_target="tpu_custom_call" | custom-call | flops 1024 | bytes 1024 | tf_op jit(solution)/shard_map/pallas_call | solution.py:252
  12.0 0.1 collective-permute-start
  12.1 0.4 %collective-permute-done.1.rows_ref = bf16[128,2048]{1,0:T(8,128)(2,1)S(1)} collective-permute-done((bf16[128,2048]{1,0:T(8,128)(2,1)S(1)}, bf16[128,2048]{1,0:T(8,128)(2,1)S(1)}, u32[]{:S(2)}, u32[]{:S(2)}) %collective-permute-start.1) | collective-permute-done | bytes 524320 | tf_op jit(solution)/shard_map/ppermute | solution.py:238
  12.5 3.1 %collective-permute-start.3 = (bf16[128,2048]{1,0:T(8,128)(2,1)S(1)}, bf16[128,2048]{1,0:T(8,128)(2,1)S(1)}, u32[]{:S(2)}, u32[]{:S(2)}) collective-permute-start(bf16[128,2048]{1,0:T(8,128)(2,1)S(1)} %collective-permute-done.1.rows_ref), channel_id=1, source_target_pairs={{4,6},{5,7},{6,4},{7,5},{8,9},{9,8},{10,11},{11,10},{12,14},{13,15... | collective-permute-start | bytes 1572872 | tf_op jit(solution)/shard_map/ppermute | solution.py:262
  15.7 2.5 %shard_map.40.own_ref = f32[1,512]{1,0:T(1,128)S(1)} custom-call(bf16[520,2048]{1,0:T(8,128)(2,1)S(1)} %get-tuple-element.17.whole_ref, bf16[1024,2048]{1,0:T(8,128)(2,1)S(1)} %get-tuple-element.18.peptides_ref), custom_call_target="tpu_custom_call" | custom-call | flops 34359738368 | bytes 1024 | tf_op jit(solution)/shard_map/pallas_call | solution.py:260
  18.2 0.5 %shard_map.41.direct_ref = bf16[128,2048]{1,0:T(8,128)(2,1)S(1)} custom-call(bf16[128,2048]{1,0:T(8,128)(2,1)S(1)} %collective-permute-done.1.rows_ref), custom_call_target="tpu_custom_call" | custom-call | flops 1024 | bytes 1024 | tf_op jit(solution)/shard_map/pallas_call | solution.py:263
  18.7 0.0 collective-permute-done.whole_ref
  18.7 2.5 %shard_map.42 = f32[1,512]{1,0:T(1,128)S(1)} custom-call(bf16[520,2048]{1,0:T(8,128)(2,1)S(1)} %collective-permute-done.whole_ref, bf16[1024,2048]{1,0:T(8,128)(2,1)S(1)} %get-tuple-element.18.peptides_ref), custom_call_target="tpu_custom_call" | custom-call | flops 1024 | bytes 1024 | tf_op jit(solution)/shard_map/pallas_call | solution.py:265
  21.3 0.1 collective-permute-start.4
  21.3 1.1 %collective-permute-done.3.rows_ref = bf16[128,2048]{1,0:T(8,128)(2,1)S(1)} collective-permute-done((bf16[128,2048]{1,0:T(8,128)(2,1)S(1)}, bf16[128,2048]{1,0:T(8,128)(2,1)S(1)}, u32[]{:S(2)}, u32[]{:S(2)}) %collective-permute-start.3) | collective-permute-done | bytes 524320 | tf_op jit(solution)/shard_map/ppermute | solution.py:262
  22.4 0.5 %shard_map.43.relayed_ref = bf16[128,2048]{1,0:T(8,128)(2,1)S(1)} custom-call(bf16[128,2048]{1,0:T(8,128)(2,1)S(1)} %collective-permute-done.3.rows_ref), custom_call_target="tpu_custom_call" | custom-call | flops 1024 | bytes 1024 | tf_op jit(solution)/shard_map/pallas_call | solution.py:268
  22.9 1.2 %collective-permute-done.2.middle_ref = bf16[264,2048]{1,0:T(8,128)(2,1)S(1)} collective-permute-done((bf16[264,2048]{1,0:T(8,128)(2,1)S(1)}, bf16[264,2048]{1,0:T(8,128)(2,1)S(1)}, u32[]{:S(2)}, u32[]{:S(2)}) %collective-permute-start.2) | collective-permute-done | bytes 1081376 | tf_op jit(solution)/shard_map/ppermute | solution.py:251
  24.2 0.0 collective-permute-done.4.back_ref
  24.2 1.4 %shard_map.44 = f32[8,512]{1,0:T(8,128)S(1)} custom-call(bf16[128,2048]{1,0:T(8,128)(2,1)S(1)} %shard_map.41.direct_ref, bf16[128,2048]{1,0:T(8,128)(2,1)S(1)} %shard_map.43.relayed_ref, bf16[264,2048]{1,0:T(8,128)(2,1)S(1)} %collective-permute-done.2.middle_ref, bf16[1024,2048]{1,0:T(8,128)(2,1)S(1)} %get-tuple-element.18.peptides_ref, ...), custom_call_target="tpu_custom_call" | custom-call | flops 1024 | bytes 1024 | tf_op jit(solution)/shard_map/pallas_call | solution.py:271
  25.6 10.0 %all_to_all.9 = f32[8,1,512]{2,1,0:T(1,128)S(1)} all-to-all(f32[8,1,512]{2,1,0:T(1,128)S(1)} %copy.4), channel_id=1, replica_groups={{4,5,6,7,8,9,10,11},{12,13,14,15,16,17,18,19},{20,21,22,23,24,25,26,27}..., dimensions={0} | all-to-all | bytes 32768 | tf_op jit(solution)/shard_map/all_to_all | solution.py:277
  35.6 0.6 %reduce_max.9 = f32[512]{0:T(512)} reduce(f32[8,1,512]{2,1,0:T(1,128)S(1)} %all_to_all.9, f32[]{:T(128)} %constant.0.clone.1), dimensions={0,1}, to_apply=%region_0.0 | reduce | flops 3584 | bytes 18436 | tf_op jit(solution)/shard_map/reduce_max | solution.py:278
  (1 shorter events, 0.0 us)
Async XLA Ops:
  1.1 11.5 %collective-permute-start.1 = (bf16[128,2048]{1,0:T(8,128)(2,1)S(1)}, bf16[128,2048]{1,0:T(8,128)(2,1)S(1)}, u32[]{:S(2)}, u32[]{:S(2)}) collective-permute-start(bf16[128,2048]{1,0:T(8,128)(2,1)S(1)} %shard_map.37.quarter_ref), channel_id=1, source_target_pairs={{4,8},{12,16},{20,24},{8,4},{16,12},{24,20},{5,9},{13,17},{21,25},... | collective-permute-start | bytes 1572872 | tf_op jit(solution)/shard_map/ppermute | solution.py:238
  7.7 16.5 %collective-permute-start.2 = (bf16[264,2048]{1,0:T(8,128)(2,1)S(1)}, bf16[264,2048]{1,0:T(8,128)(2,1)S(1)}, u32[]{:S(2)}, u32[]{:S(2)}) collective-permute-start(bf16[264,2048]{1,0:T(8,128)(2,1)S(1)} %shard_map.38.middle_ref), channel_id=1, source_target_pairs={{4,8},{12,16},{20,24},{8,4},{16,12},{24,20},{5,9},{13,17},{21,25},... | collective-permute-start | bytes 3244040 | tf_op jit(solution)/shard_map/ppermute | solution.py:251
  12.0 6.7 %collective-permute-start = (bf16[520,2048]{1,0:T(8,128)(2,1)S(1)}, bf16[520,2048]{1,0:T(8,128)(2,1)S(1)}, u32[]{:S(2)}, u32[]{:S(2)}) collective-permute-start(bf16[520,2048]{1,0:T(8,128)(2,1)S(1)} %get-tuple-element.17.whole_ref), channel_id=1, source_target_pairs={{0,4},{4,0},{8,12},{12,8},{16,20},{20,16},{24,28},{28,24},{1,5},{5... | collective-permute-start | bytes 6389768 | tf_op jit(solution)/shard_map/ppermute | solution.py:261
  12.5 9.9 %collective-permute-start.3 = (bf16[128,2048]{1,0:T(8,128)(2,1)S(1)}, bf16[128,2048]{1,0:T(8,128)(2,1)S(1)}, u32[]{:S(2)}, u32[]{:S(2)}) collective-permute-start(bf16[128,2048]{1,0:T(8,128)(2,1)S(1)} %collective-permute-done.1.rows_ref), channel_id=1, source_target_pairs={{4,6},{5,7},{6,4},{7,5},{8,9},{9,8},{10,11},{11,10},{12,14},{13,15... | collective-permute-start | bytes 1572872 | tf_op jit(solution)/shard_map/ppermute | solution.py:262
  21.3 2.9 %collective-permute-start.4 = (f32[1,512]{1,0:T(1,128)S(1)}, f32[1,512]{1,0:T(1,128)S(1)}, u32[]{:S(2)}, u32[]{:S(2)}) collective-permute-start(f32[1,512]{1,0:T(1,128)S(1)} %shard_map.42), channel_id=1, source_target_pairs={{0,4},{4,0},{8,12},{12,8},{16,20},{20,16},{24,28},{28,24},{1,5},{5... | collective-permute-start | bytes 6152 | tf_op jit(solution)/shard_map/ppermute | solution.py:266

commit v8 on v7

--- a/solution.py
+++ b/solution.py
@@ -12,7 +12,7 @@
 HBM = pl.BlockSpec(memory_space=pltpu.HBM)
 BLOCK = 256
 PAD = 128
-NOTE = 8
+NOTE = 16
 LONG = 2**35
 DIGITS = 3
 

time: 36.5 us -> 36.8 us (level)
  no operation moved by 1% of the time
where the time goes in v8:
time: 36.8 us; the launch traced here: 36.6 us
  Pallas kernels  12.9 us (35%)
  blocking collectives  10 us (27%)
  starting transfers between devices  9.79 us (27%)
  waiting for transfers between devices  3.07 us (8%)
  other arithmetic  0.61 us (2%)
    all_to_all x1, blocking collectives, per_device(): lax.all_to_all(bests, ('mass', 'pep'), 0, 0, axis_index_groups=groups)  10 us
    ppermute x1, starting transfers between devices, per_device(): direct = lax.ppermute(quarter, 'mass', across)  4.59 us
    ppermute x1, starting transfers between devices, per_device(): relayed = lax.ppermute(direct, ('mass', 'pep'), relay)  3.14 us
    pallas_call x1, Pallas kernels, per_device(): own_best, = call(near_kernel, *score, LONG)(whole, held)  2.54 us
    pallas_call x1, Pallas kernels, per_device(): near_best, = call(near_kernel, *score)(near, held)  2.54 us
    pallas_call x1, Pallas kernels, per_device(): call(whole_kernel, [((rows + NOTE, bins), bf16), (peptides.shape, bf16)],...  2.4 us
    pallas_call x1, Pallas kernels, per_device(): call(middle_kernel, [((rows - 2 * part + NOTE, bins), bf16)], [HBM, HBM],...  2.03 us
    ppermute x1, starting transfers between devices, per_device(): far = lax.ppermute(middle, 'mass', across)  1.92 us
  transfers between devices with their start and end apart: 5, of which 3 were waited for; matrix products, arithmetic and copies ran while one was open for 0% of the time, Pallas kernels for 29%

profile of v8, /device:TPU:1, one launch (start us, length us, event | category | flops | bytes accessed | tf_op | source)
XLA Modules:
  0.0 36.6 jit_solution(9129776608870672098)
XLA Ops:
  0.0 1.0 %shard_map.37.quarter_ref = bf16[128,2048]{1,0:T(8,128)(2,1)S(1)} custom-call(bf16[512,2048]{1,0:T(8,128)(2,1)} %spectra_ref.5), custom_call_target="tpu_custom_call" | custom-call | flops 1024 | bytes 1024 | tf_op jit(solution)/shard_map/pallas_call | solution.py:232
  1.1 4.6 %collective-permute-start.1 = (bf16[128,2048]{1,0:T(8,128)(2,1)S(1)}, bf16[128,2048]{1,0:T(8,128)(2,1)S(1)}, u32[]{:S(2)}, u32[]{:S(2)}) collective-permute-start(bf16[128,2048]{1,0:T(8,128)(2,1)S(1)} %shard_map.37.quarter_ref), channel_id=1, source_target_pairs={{4,8},{12,16},{20,24},{8,4},{16,12},{24,20},{5,9},{13,17},{21,25},... | collective-permute-start | bytes 1572872 | tf_op jit(solution)/shard_map/ppermute | solution.py:238
  5.7 2.0 %shard_map.38.middle_ref = bf16[272,2048]{1,0:T(8,128)(2,1)S(1)} custom-call(bf16[512,2048]{1,0:T(8,128)(2,1)} %spectra_ref.5, s32[2,512]{1,0:T(2,128)} %bitcast.3), custom_call_target="tpu_custom_call" | custom-call | flops 1024 | bytes 1024 | tf_op jit(solution)/shard_map/pallas_call | solution.py:241
  7.7 1.9 %collective-permute-start.2 = (bf16[272,2048]{1,0:T(8,128)(2,1)S(1)}, bf16[272,2048]{1,0:T(8,128)(2,1)S(1)}, u32[]{:S(2)}, u32[]{:S(2)}) collective-permute-start(bf16[272,2048]{1,0:T(8,128)(2,1)S(1)} %shard_map.38.middle_ref), channel_id=1, source_target_pairs={{4,8},{12,16},{20,24},{8,4},{16,12},{24,20},{5,9},{13,17},{21,25},... | collective-permute-start | bytes 3342344 | tf_op jit(solution)/shard_map/ppermute | solution.py:251
  9.6 2.4 %shard_map.39 = (bf16[528,2048]{1,0:T(8,128)(2,1)S(1)}, bf16[1024,2048]{1,0:T(8,128)(2,1)S(1)}) custom-call(bf16[512,2048]{1,0:T(8,128)(2,1)} %spectra_ref.5, bf16[1024,2048]{1,0:T(8,128)(2,1)} %peptides_ref.1, bf16[128,2048]{1,0:T(8,128)(2,1)S(1)} %shard_map.37.quarter_ref, bf16[272,2048]{1,0:T(8,128)(2,1)S(1)} %shard_map.38.middle_ref), custom_call_target="tpu_custom_call" | custom-call | flops 1024 | bytes 1024 | tf_op jit(solution)/shard_map/pallas_call | solution.py:252
  12.0 0.1 collective-permute-start
  12.1 0.4 %collective-permute-done.1.rows_ref = bf16[128,2048]{1,0:T(8,128)(2,1)S(1)} collective-permute-done((bf16[128,2048]{1,0:T(8,128)(2,1)S(1)}, bf16[128,2048]{1,0:T(8,128)(2,1)S(1)}, u32[]{:S(2)}, u32[]{:S(2)}) %collective-permute-start.1) | collective-permute-done | bytes 524320 | tf_op jit(solution)/shard_map/ppermute | solution.py:238
  12.5 3.1 %collective-permute-start.3 = (bf16[128,2048]{1,0:T(8,128)(2,1)S(1)}, bf16[128,2048]{1,0:T(8,128)(2,1)S(1)}, u32[]{:S(2)}, u32[]{:S(2)}) collective-permute-start(bf16[128,2048]{1,0:T(8,128)(2,1)S(1)} %collective-permute-done.1.rows_ref), channel_id=1, source_target_pairs={{4,6},{5,7},{6,4},{7,5},{8,9},{9,8},{10,11},{11,10},{12,14},{13,15... | collective-permute-start | bytes 1572872 | tf_op jit(solution)/shard_map/ppermute | solution.py:262
  15.7 2.5 %shard_map.40.own_ref = f32[1,512]{1,0:T(1,128)S(1)} custom-call(bf16[528,2048]{1,0:T(8,128)(2,1)S(1)} %get-tuple-element.17.whole_ref, bf16[1024,2048]{1,0:T(8,128)(2,1)S(1)} %get-tuple-element.18.peptides_ref), custom_call_target="tpu_custom_call" | custom-call | flops 34359738368 | bytes 1024 | tf_op jit(solution)/shard_map/pallas_call | solution.py:260
  18.2 0.5 %shard_map.41.direct_ref = bf16[128,2048]{1,0:T(8,128)(2,1)S(1)} custom-call(bf16[128,2048]{1,0:T(8,128)(2,1)S(1)} %collective-permute-done.1.rows_ref), custom_call_target="tpu_custom_call" | custom-call | flops 1024 | bytes 1024 | tf_op jit(solution)/shard_map/pallas_call | solution.py:263
  18.7 0.0 collective-permute-done.whole_ref
  18.7 2.5 %shard_map.42 = f32[1,512]{1,0:T(1,128)S(1)} custom-call(bf16[528,2048]{1,0:T(8,128)(2,1)S(1)} %collective-permute-done.whole_ref, bf16[1024,2048]{1,0:T(8,128)(2,1)S(1)} %get-tuple-element.18.peptides_ref), custom_call_target="tpu_custom_call" | custom-call | flops 1024 | bytes 1024 | tf_op jit(solution)/shard_map/pallas_call | solution.py:265
  21.3 0.1 collective-permute-start.4
  21.3 1.1 %collective-permute-done.3.rows_ref = bf16[128,2048]{1,0:T(8,128)(2,1)S(1)} collective-permute-done((bf16[128,2048]{1,0:T(8,128)(2,1)S(1)}, bf16[128,2048]{1,0:T(8,128)(2,1)S(1)}, u32[]{:S(2)}, u32[]{:S(2)}) %collective-permute-start.3) | collective-permute-done | bytes 524320 | tf_op jit(solution)/shard_map/ppermute | solution.py:262
  22.4 0.5 %shard_map.43.relayed_ref = bf16[128,2048]{1,0:T(8,128)(2,1)S(1)} custom-call(bf16[128,2048]{1,0:T(8,128)(2,1)S(1)} %collective-permute-done.3.rows_ref), custom_call_target="tpu_custom_call" | custom-call | flops 1024 | bytes 1024 | tf_op jit(solution)/shard_map/pallas_call | solution.py:268
  22.9 1.6 %collective-permute-done.2.middle_ref = bf16[272,2048]{1,0:T(8,128)(2,1)S(1)} collective-permute-done((bf16[272,2048]{1,0:T(8,128)(2,1)S(1)}, bf16[272,2048]{1,0:T(8,128)(2,1)S(1)}, u32[]{:S(2)}, u32[]{:S(2)}) %collective-permute-start.2) | collective-permute-done | bytes 1114144 | tf_op jit(solution)/shard_map/ppermute | solution.py:251
  24.5 0.0 collective-permute-done.4.back_ref
  24.5 1.4 %shard_map.44 = f32[8,512]{1,0:T(8,128)S(1)} custom-call(bf16[128,2048]{1,0:T(8,128)(2,1)S(1)} %shard_map.41.direct_ref, bf16[128,2048]{1,0:T(8,128)(2,1)S(1)} %shard_map.43.relayed_ref, bf16[272,2048]{1,0:T(8,128)(2,1)S(1)} %collective-permute-done.2.middle_ref, bf16[1024,2048]{1,0:T(8,128)(2,1)S(1)} %get-tuple-element.18.peptides_ref, ...), custom_call_target="tpu_custom_call" | custom-call | flops 1024 | bytes 1024 | tf_op jit(solution)/shard_map/pallas_call | solution.py:271
  25.9 10.0 %all_to_all.9 = f32[8,1,512]{2,1,0:T(1,128)S(1)} all-to-all(f32[8,1,512]{2,1,0:T(1,128)S(1)} %copy.4), channel_id=1, replica_groups={{4,5,6,7,8,9,10,11},{12,13,14,15,16,17,18,19},{20,21,22,23,24,25,26,27}..., dimensions={0} | all-to-all | bytes 32768 | tf_op jit(solution)/shard_map/all_to_all | solution.py:277
  36.0 0.6 %reduce_max.9 = f32[512]{0:T(512)} reduce(f32[8,1,512]{2,1,0:T(1,128)S(1)} %all_to_all.9, f32[]{:T(128)} %constant.0.clone.1), dimensions={0,1}, to_apply=%region_0.0 | reduce | flops 3584 | bytes 18436 | tf_op jit(solution)/shard_map/reduce_max | solution.py:278
  (1 shorter events, 0.0 us)
Async XLA Ops:
  1.1 11.5 %collective-permute-start.1 = (bf16[128,2048]{1,0:T(8,128)(2,1)S(1)}, bf16[128,2048]{1,0:T(8,128)(2,1)S(1)}, u32[]{:S(2)}, u32[]{:S(2)}) collective-permute-start(bf16[128,2048]{1,0:T(8,128)(2,1)S(1)} %shard_map.37.quarter_ref), channel_id=1, source_target_pairs={{4,8},{12,16},{20,24},{8,4},{16,12},{24,20},{5,9},{13,17},{21,25},... | collective-permute-start | bytes 1572872 | tf_op jit(solution)/shard_map/ppermute | solution.py:238
  7.7 16.8 %collective-permute-start.2 = (bf16[272,2048]{1,0:T(8,128)(2,1)S(1)}, bf16[272,2048]{1,0:T(8,128)(2,1)S(1)}, u32[]{:S(2)}, u32[]{:S(2)}) collective-permute-start(bf16[272,2048]{1,0:T(8,128)(2,1)S(1)} %shard_map.38.middle_ref), channel_id=1, source_target_pairs={{4,8},{12,16},{20,24},{8,4},{16,12},{24,20},{5,9},{13,17},{21,25},... | collective-permute-start | bytes 3342344 | tf_op jit(solution)/shard_map/ppermute | solution.py:251
  12.0 6.7 %collective-permute-start = (bf16[528,2048]{1,0:T(8,128)(2,1)S(1)}, bf16[528,2048]{1,0:T(8,128)(2,1)S(1)}, u32[]{:S(2)}, u32[]{:S(2)}) collective-permute-start(bf16[528,2048]{1,0:T(8,128)(2,1)S(1)} %get-tuple-element.17.whole_ref), channel_id=1, source_target_pairs={{0,4},{4,0},{8,12},{12,8},{16,20},{20,16},{24,28},{28,24},{1,5},{5... | collective-permute-start | bytes 6488072 | tf_op jit(solution)/shard_map/ppermute | solution.py:261
  12.5 9.9 %collective-permute-start.3 = (bf16[128,2048]{1,0:T(8,128)(2,1)S(1)}, bf16[128,2048]{1,0:T(8,128)(2,1)S(1)}, u32[]{:S(2)}, u32[]{:S(2)}) collective-permute-start(bf16[128,2048]{1,0:T(8,128)(2,1)S(1)} %collective-permute-done.1.rows_ref), channel_id=1, source_target_pairs={{4,6},{5,7},{6,4},{7,5},{8,9},{9,8},{10,11},{11,10},{12,14},{13,15... | collective-permute-start | bytes 1572872 | tf_op jit(solution)/shard_map/ppermute | solution.py:262
  21.3 3.3 %collective-permute-start.4 = (f32[1,512]{1,0:T(1,128)S(1)}, f32[1,512]{1,0:T(1,128)S(1)}, u32[]{:S(2)}, u32[]{:S(2)}) collective-permute-start(f32[1,512]{1,0:T(1,128)S(1)} %shard_map.42), channel_id=1, source_target_pairs={{0,4},{4,0},{8,12},{12,8},{16,20},{20,16},{24,28},{28,24},{1,5},{5... | collective-permute-start | bytes 6152 | tf_op jit(solution)/shard_map/ppermute | solution.py:266
